TPU v7x, 256 devices: a whole 4x4x8 slice. The times are simulated.
256 devices in a mesh: ctx: 32 (over x, z), expert: 8 (over y, core).
Axes of the slice: x: 4, y: 4, z: 8, core: 2. Of those that a mesh axis runs over, the one named last changes fastest.
Arguments:
- latent_plane: bfloat16 [128, 2048, 512], P('ctx', 'expert'), may hold values from -64 to 64
- latent_rope: bfloat16 [128, 131072], P('ctx', 'expert'), may hold values from -7 to 7
- query_plane: bfloat16 [128, 128, 512], P('ctx', 'expert'), may hold values from -16 to 16
- query_rope: bfloat16 [128, 8192], P('ctx', 'expert'), may hold values from -32 to 32
- decode_hidden: bfloat16 [128, 7168], P('ctx', 'expert'), may hold values from -6 to 6
- lengths: int32 [32, 4], P('ctx'), may hold values from 128 to 2048, as said below
- owner: int32 [32, 4], P('ctx'), may hold values from 0 to 31, as said below
- norm_gain: float32 [7168], P('expert'), may hold values from 0.1 to 1.9
- routes: int32 [128, 8], P('ctx'), may hold values from 0 to 31, all different within a row; in each aligned block of 4 rows (0 to 3, 4 to 7, ...) at most 3 rows name the same one
- combine: float32 [128, 8], P('ctx'), may hold values from 0.1 to 1
- gate_weight: bfloat16 [32, 7168, 2048], P('ctx', None, 'expert'), may hold values from -0.0625 to 0.0625
- up_weight: bfloat16 [32, 7168, 2048], P('ctx', None, 'expert'), may hold values from -0.0625 to 0.0625
- down_weight: bfloat16 [32, 2048, 7168], P('ctx', 'expert'), may hold values from -0.125 to 0.125
Outputs:
- attended: bfloat16 [128, 65536], P('ctx', 'expert')
- moe_out: bfloat16 [128, 7168], P('ctx', 'expert')
Inputs may be any that keep to these rules, and one draw needn't show every extreme that they name: Each row names 4 different owners, and every owner receives exactly 4 requests. `lengths`: each row sums to 4096, and its largest entry is 2048. `routes`: each row names 8 different experts; within the rows of one index of ctx no expert is named more than 3 times, and some expert reaches 3.
All inputs are finite; a program needn't handle non-finite values.
Results may differ from a plain program's by a relative error of at most 0.0091.
Values may be sent and summed in bfloat16 or wider, within the bound.
A program may use at most 128 MiB of HBM per device.

v0:
```python
import jax
import jax.numpy as jnp
from jax import lax
from jax.sharding import PartitionSpec as P

D = 7168
ROPE = 64
TOPK = 8
BLK = 128


score_scale = 192.0 ** (-0.5)
pack_limit = 448.0


def expert_block(rows_in, gate_weight, up_weight, down_weight):
    owners = rows_in.shape[0]
    items = rows_in.shape[1]
    flattened = rows_in.reshape(owners * items, rows_in.shape[2])
    gate_act = jnp.dot(flattened, gate_weight[0], preferred_element_type=jnp.float32)
    up_act = jnp.dot(flattened, up_weight[0], preferred_element_type=jnp.float32)
    hidden = (jax.nn.silu(gate_act) * up_act).astype(jnp.bfloat16)
    projected = jnp.dot(hidden, down_weight[0], preferred_element_type=jnp.float32).reshape(
        owners, items, -1
    )
    summed = lax.psum_scatter(projected, "expert", scatter_dimension=2, tiled=True)
    return lax.all_to_all(
        summed.astype(jnp.bfloat16), "ctx", split_axis=0, concat_axis=0, tiled=True
    )


def local(
    latent_plane,
    latent_rope,
    query_plane,
    query_rope,
    decode_hidden,
    lengths,
    owner,
    norm_gain,
    routes,
    combine,
    gate_weight,
    up_weight,
    down_weight,
):
    request_count = latent_plane.shape[0]
    rows_dev = latent_plane.shape[1]
    latent_width = latent_plane.shape[2]
    heads_dev = query_plane.shape[1]
    block_count = latent_width // BLK
    owners = lax.axis_size("ctx")
    column = lax.axis_index("expert")
    blocks = latent_plane.astype(jnp.float32).reshape(request_count, rows_dev, block_count, BLK)
    scales = ((jnp.max(jnp.abs(blocks), axis=-1) + 1e-06) / pack_limit).astype(jnp.bfloat16)
    packed = (blocks / scales.astype(jnp.float32)[..., None]).astype(jnp.bfloat16)
    positions = column * rows_dev + jnp.arange(rows_dev, dtype=jnp.int32)
    visible = (positions[None, :] < lengths[0][:, None]).astype(jnp.bfloat16)
    routing = (owner[0][None, :] == jnp.arange(owners, dtype=jnp.int32)[:, None]).astype(
        jnp.bfloat16
    )

    def spread(values):
        return jnp.dot(
            routing, values.reshape(request_count, -1), preferred_element_type=jnp.float32
        ).astype(jnp.bfloat16)

    occupied_sent = jnp.sum(routing.astype(jnp.float32), axis=1, keepdims=True).astype(jnp.bfloat16)
    received = (
        lax.all_to_all(spread(packed), "ctx", split_axis=0, concat_axis=0, tiled=True),
        lax.all_to_all(spread(scales), "ctx", split_axis=0, concat_axis=0, tiled=True),
        lax.all_to_all(spread(latent_rope), "ctx", split_axis=0, concat_axis=0, tiled=True),
        lax.all_to_all(spread(visible), "ctx", split_axis=0, concat_axis=0, tiled=True),
        lax.all_to_all(occupied_sent, "ctx", split_axis=0, concat_axis=0, tiled=True),
    )
    occupied = received[4][:, 0].astype(jnp.float32)
    ranking = jnp.cumsum(occupied) - occupied
    select = (
        (ranking[None, :] == jnp.arange(request_count, dtype=jnp.float32)[:, None])
        & (occupied[None, :] > 0.5)
    ).astype(jnp.bfloat16)

    def own_rows(values):
        return jnp.dot(select, values, preferred_element_type=jnp.float32).astype(jnp.bfloat16)

    packed_own = own_rows(received[0]).reshape(request_count, rows_dev, block_count, BLK)
    scales_own = own_rows(received[1]).reshape(request_count, rows_dev, block_count)
    key_rows = (
        (packed_own.astype(jnp.float32) * scales_own.astype(jnp.float32)[..., None])
        .reshape(request_count, rows_dev, latent_width)
        .astype(jnp.bfloat16)
    )
    rope_rows = own_rows(received[2]).reshape(request_count, rows_dev, ROPE)
    seen_own = own_rows(received[3])
    query_rot = query_rope.reshape(request_count, heads_dev, ROPE)
    all_keys, all_rope, all_seen = (
        lax.all_gather(key_rows, "expert", axis=1, tiled=True),
        lax.all_gather(rope_rows, "expert", axis=1, tiled=True),
        lax.all_gather(seen_own, "expert", axis=1, tiled=True),
    )
    scores = jnp.einsum("rhc,rpc->rhp", query_plane, all_keys, preferred_element_type=jnp.float32)
    scores = scores + jnp.einsum(
        "rhe,rpe->rhp", query_rot, all_rope, preferred_element_type=jnp.float32
    )
    scores = scores * score_scale
    seen_mask = (all_seen > 0.5)[:, None, :]
    masked = jnp.where(seen_mask, scores, -jnp.inf)
    highest = jnp.max(masked, axis=-1, keepdims=True)
    exponent = jnp.where(seen_mask, jnp.exp(masked - highest), 0.0)
    totals = jnp.sum(exponent, axis=-1, keepdims=True)
    probs = (exponent / totals).astype(jnp.bfloat16)
    attended = jnp.einsum(
        "rhp,rpc->rhc", probs, all_keys, preferred_element_type=jnp.float32
    ).astype(jnp.bfloat16)
    attended = attended.reshape(request_count, heads_dev * latent_width)
    stateful = decode_hidden.astype(jnp.float32)
    squares = lax.psum(jnp.sum(stateful * stateful, axis=-1), "expert")
    normed = (stateful * lax.rsqrt(squares / D + 1e-06)[:, None] * norm_gain[None, :]).astype(
        jnp.bfloat16
    )
    capacity = min(request_count, request_count * TOPK // owners + 2)
    choice_count = request_count * TOPK
    chosen_ids = routes.reshape(choice_count)
    chosen_weights = combine.reshape(choice_count)
    experts_seen = (chosen_ids[:, None] == jnp.arange(owners, dtype=jnp.int32)[None, :]).astype(
        jnp.float32
    )
    choice_index = jnp.arange(choice_count, dtype=jnp.int32)
    earlier = (choice_index[:, None] > choice_index[None, :]).astype(jnp.float32)
    counts = jnp.dot(earlier, experts_seen, precision=lax.Precision.HIGHEST)
    slot_index = jnp.sum(counts * experts_seen, axis=1).astype(jnp.int32)
    destination = chosen_ids * capacity + slot_index
    dispatch = (
        jnp.arange(owners * capacity, dtype=jnp.int32)[:, None] == destination[None, :]
    ).astype(jnp.float32)
    token_of = (
        (choice_index // TOPK)[:, None] == jnp.arange(request_count, dtype=jnp.int32)[None, :]
    ).astype(jnp.float32)
    placing = jnp.dot(dispatch, token_of, precision=lax.Precision.HIGHEST).astype(jnp.bfloat16)
    weight_map = jnp.dot(
        token_of.T, dispatch.T * chosen_weights[:, None], precision=lax.Precision.HIGHEST
    )
    whole_rows = lax.all_gather(normed, "expert", axis=1, tiled=True)
    outgoing = (
        jnp.dot(placing, whole_rows, preferred_element_type=jnp.float32)
        .astype(jnp.bfloat16)
        .reshape(owners, capacity, -1)
    )
    returned = expert_block(
        lax.all_to_all(outgoing, "ctx", split_axis=0, concat_axis=0, tiled=True),
        gate_weight,
        up_weight,
        down_weight,
    )
    flat_returned = returned.reshape(owners * capacity, -1).astype(jnp.float32)
    moe_out = jnp.dot(weight_map, flat_returned, precision=lax.Precision.HIGHEST).astype(
        jnp.bfloat16
    )
    return (attended, moe_out)


def solution(mesh):
    placed = (
        P("ctx", "expert", None),
        P("ctx", "expert"),
        P("ctx", "expert", None),
        P("ctx", "expert"),
        P("ctx", "expert"),
        P("ctx", None),
        P("ctx", None),
        P("expert"),
        P("ctx", None),
        P("ctx", None),
        P("ctx", None, "expert"),
        P("ctx", None, "expert"),
        P("ctx", "expert", None),
    )
    return jax.shard_map(
        local,
        mesh=mesh,
        in_specs=placed,
        out_specs=(P("ctx", "expert"), P("ctx", "expert")),
        check_vma=False,
    )
```

profile of v0, /device:TPU:1, one launch (start us, length us, event | category | flops | bytes accessed | tf_op | source)
XLA Modules:
  0.0 468.1 jit_solution(12157213219373837717)
XLA Ops:
  7.2 0.8 fusion.55
  8.7 11.9 %all-to-all-start = ((bf16[32,1,1]{2,1,0:T(2,128)(2,1)}), bf16[32,1,1]{2,1,0:T(2,128)(2,1)S(1)}, u32[]{:S(2)}, u32[]{:S(2)}) async-start(bf16[32,1,1]{2,1,0:T(2,128)(2,1)} %copy.40), calls=%async_computation | async-start | bytes 32768 | tf_op jit(solution)/shard_map/all_to_all | solution.py:74
  20.5 2.9 convert_abs_fusion
  23.4 1.9 abs.7
  25.4 1.1 reduce_max.18
  27.6 12.9 %psum.7 = f32[4]{0:T(128)S(1)} all-reduce(f32[4]{0:T(128)S(1)} %fusion.41), channel_id=1, replica_groups=mesh['ctx'=32,'expert'=8] {'expert'}, use_global_device_ids=true, to_apply=%region_7.8 | all-reduce | flops 4 | bytes 32 | tf_op jit(solution)/shard_map/psum | solution.py:117
  40.6 15.2 %all_gather.15 = bf16[4,7168]{1,0:T(4,128)(2,1)S(1)} all-gather(bf16[4,896]{1,0:T(4,128)(2,1)S(1)} %fusion.43), channel_id=1, replica_groups=mesh['ctx'=32,'expert'=8] {'expert'}, dimensions={1}, use_global_device_ids=true | all-gather | bytes 64512 | tf_op jit(solution)/shard_map/all_gather | solution.py:143
  57.9 9.2 %all-to-all-start.3 = ((bf16[32,2,512]{2,1,0:T(2,128)(2,1)}), bf16[32,2,512]{2,1,0:T(2,128)(2,1)S(1)}, u32[]{:S(2)}, u32[]{:S(2)}) async-start(bf16[32,2,512]{2,1,0:T(2,128)(2,1)} %reshape.179), calls=%async_computation.3 | async-start | bytes 131072 | tf_op jit(solution)/shard_map/all_to_all | solution.py:71
  67.7 2.2 reshape.169
  69.9 6.1 %all-to-all-done.3 = bf16[32,2,512]{2,1,0:T(2,128)(2,1)S(1)} async-done(((bf16[32,2,512]{2,1,0:T(2,128)(2,1)}), bf16[32,2,512]{2,1,0:T(2,128)(2,1)S(1)}, u32[]{:S(2)}, u32[]{:S(2)}) %all-to-all-start.3) | async-done | bytes 65568 | tf_op jit(solution)/shard_map/all_to_all | solution.py:71
  76.0 5.1 %all-to-all-start.5 = ((bf16[32,3,7168]{2,1,0:T(4,128)(2,1)}), bf16[32,3,7168]{2,1,0:T(4,128)(2,1)}, u32[]{:S(2)}, u32[]{:S(2)}) async-start(bf16[32,3,7168]{2,1,0:T(4,128)(2,1)} %reshape.169), calls=%async_computation.5 | async-start | bytes 3670016 | tf_op jit(solution)/shard_map/all_to_all | solution.py:150
  81.1 1.2 div.44
  82.4 2.7 div.45
  85.4 1.4 copy.53
  87.0 4.7 %fusion.1 = bf16[32,1,131072]{2,0,1:T(8,128)(2,1)} fusion(f32[4,131072]{1,0:T(4,128)S(1)} %bitcast.71, f32[4,131072]{1,0:T(4,128)S(1)} %copy-done.4, s32[4]{0:T(128)S(1)} %bitcast.76), kind=kOutput, calls=%fused_computation.2 | convolution fusion | flops 38797440 | bytes 12582928 | tf_op jit(solution)/shard_map/dot_general | solution.py:64
  91.7 11.5 %reduce.5 = bf16[32,131072]{1,0:T(8,128)(2,1)} reduce(bf16[32,1,131072]{2,0,1:T(8,128)(2,1)} %fusion.1, bf16[]{:T(256)} %broadcast.99), dimensions={1}, to_apply=%copy.43.reduce_sub_computation | reduce | bytes 16777218 | tf_op jit(solution)/shard_map/all_to_all | solution.py:70
  103.2 11.0 %reshape.181 = bf16[32,2,65536]{2,1,0:T(2,128)(2,1)} reshape(bf16[32,131072]{1,0:T(8,128)(2,1)} %reduce.5) | data formatting | bytes 16777216
  114.2 9.9 %all-to-all-done.5 = bf16[32,3,7168]{2,1,0:T(4,128)(2,1)} async-done(((bf16[32,3,7168]{2,1,0:T(4,128)(2,1)}), bf16[32,3,7168]{2,1,0:T(4,128)(2,1)}, u32[]{:S(2)}, u32[]{:S(2)}) %all-to-all-start.5) | async-done | bytes 1376288 | tf_op jit(solution)/shard_map/all_to_all | solution.py:150
  124.1 7.2 %all-to-all-start.2 = ((bf16[32,2,65536]{2,1,0:T(2,128)(2,1)}), bf16[32,2,65536]{2,1,0:T(2,128)(2,1)}, u32[]{:S(2)}, u32[]{:S(2)}) async-start(bf16[32,2,65536]{2,1,0:T(2,128)(2,1)} %reshape.181), calls=%async_computation.2 | async-start | bytes 16777216 | tf_op jit(solution)/shard_map/all_to_all | solution.py:70
  131.3 11.3 %reduce-scatter.2.cloned.1.call-start = ((), (), s32[]{:S(2)}) async-start(), calls=%async_computation.10 | async-start | bytes 3096576 | tf_op jit(solution)/shard_map/reduce_scatter | solution.py:26
  142.6 3.0 reshape.170
  145.6 2.9 fusion.10
  148.7 0.7 fusion.22
  149.5 4.4 fusion.6
  155.3 1.2 mul.69
  156.5 1.9 mul.70
  158.4 156.3 %all-to-all-done.2 = bf16[32,2,65536]{2,1,0:T(2,128)(2,1)} async-done(((bf16[32,2,65536]{2,1,0:T(2,128)(2,1)}), bf16[32,2,65536]{2,1,0:T(2,128)(2,1)}, u32[]{:S(2)}, u32[]{:S(2)}) %all-to-all-start.2) | async-done | bytes 8388640 | tf_op jit(solution)/shard_map/all_to_all | solution.py:70
  314.7 23.4 %reshape.182 = bf16[32,1,131072]{2,1,0:T(2,128)(2,1)} reshape(bf16[32,2,65536]{2,1,0:T(2,128)(2,1)} %all-to-all-done.2) | data formatting | bytes 16777216
  338.1 15.0 %fusion.2 = f32[4,131072]{1,0:T(4,128)S(1)} fusion(pred[4,32]{1,0:T(4,128)(4,1)S(1)} %fusion.53, bf16[32,1,131072]{2,1,0:T(2,128)(2,1)} %reshape.182), kind=kOutput, calls=%fused_computation.4 | convolution fusion | flops 34603008 | bytes 10485888 | tf_op jit(solution)/shard_map/dot_general | solution.py:84
  353.0 1.7 fusion.18
  355.4 1.4 reduce.6
  356.8 1.6 reshape.183
  358.4 13.1 %all-to-all-start.4 = ((bf16[32,2,8192]{2,1,0:T(2,128)(2,1)}), bf16[32,2,8192]{2,1,0:T(2,128)(2,1)S(1)}, u32[]{:S(2)}, u32[]{:S(2)}) async-start(bf16[32,2,8192]{2,1,0:T(2,128)(2,1)} %reshape.183), calls=%async_computation.4 | async-start | bytes 2097152 | tf_op jit(solution)/shard_map/all_to_all | solution.py:72
  371.6 24.8 %all-to-all-done.4 = bf16[32,2,8192]{2,1,0:T(2,128)(2,1)S(1)} async-done(((bf16[32,2,8192]{2,1,0:T(2,128)(2,1)}), bf16[32,2,8192]{2,1,0:T(2,128)(2,1)S(1)}, u32[]{:S(2)}, u32[]{:S(2)}) %all-to-all-start.4) | async-done | bytes 1048608 | tf_op jit(solution)/shard_map/all_to_all | solution.py:72
  396.4 1.0 reshape.184
  397.4 1.2 convolution_convert_fusion.3
  398.9 0.8 copy.46
  401.3 8.1 %all-to-all-start.1 = ((bf16[32,2,128]{2,1,0:T(2,128)(2,1)}), bf16[32,2,128]{2,1,0:T(2,128)(2,1)S(1)}, u32[]{:S(2)}, u32[]{:S(2)}) async-start(bf16[32,2,128]{2,1,0:T(2,128)(2,1)} %reshape.185), calls=%async_computation.1 | async-start | bytes 32768 | tf_op jit(solution)/shard_map/all_to_all | solution.py:73
  409.9 8.1 %all-to-all-done.1 = bf16[32,2,128]{2,1,0:T(2,128)(2,1)S(1)} async-done(((bf16[32,2,128]{2,1,0:T(2,128)(2,1)}), bf16[32,2,128]{2,1,0:T(2,128)(2,1)S(1)}, u32[]{:S(2)}, u32[]{:S(2)}) %all-to-all-start.1) | async-done | bytes 16416 | tf_op jit(solution)/shard_map/all_to_all | solution.py:73
  418.1 13.6 %all_gather.12 = bf16[4,2048]{1,0:T(4,128)(2,1)S(1)} all-gather(bf16[4,256]{1,0:T(4,128)(2,1)S(1)} %convolution_convert_fusion.10), channel_id=1, replica_groups=mesh['ctx'=32,'expert'=8] {'expert'}, dimensions={1}, use_global_device_ids=true | all-gather | bytes 18432 | tf_op jit(solution)/shard_map/all_gather | solution.py:99
  431.8 1.0 convert_element_type.187
  432.8 0.8 copy.48
  433.6 3.9 all-to-all-start.6
  437.5 10.1 %all-to-all-done.6 = bf16[32,3,896]{2,1,0:T(4,128)(2,1)S(1)} async-done(((bf16[32,3,896]{2,1,0:T(4,128)(2,1)}), bf16[32,3,896]{2,1,0:T(4,128)(2,1)S(1)}, u32[]{:S(2)}, u32[]{:S(2)}) %all-to-all-start.6) | async-done | bytes 172064 | tf_op jit(solution)/shard_map/all_to_all | solution.py:27
  447.7 0.8 convolution_convert_fusion.9
  448.5 5.7 %fusion.64 = f32[4,2048,16]{1,2,0:T(8,128)S(1)} fusion(bf16[4,2048,512]{2,1,0:T(8,128)(2,1)} %all-gather.3.cloned.1.call-done, bf16[4,16,512]{2,1,0:T(8,128)(2,1)S(1)} %copy-done.5), kind=kOutput, calls=%fused_computation.99 | convolution fusion | flops 134217728 | bytes 8978432 | tf_op jit(solution)/shard_map/rhc,rpc->rhp/dot_general | solution.py:101
  454.2 1.5 fusion.15
  456.0 4.7 fusion.26
  (77 shorter events, 10.8 us)
Async XLA Ops:
  7.2 347.6 %copy-start = (bf16[4,16384]{1,0:T(4,128)(2,1)S(1)}, bf16[4,16384]{1,0:T(4,128)(2,1)}, u32[]{:S(2)}) copy-start(bf16[4,16384]{1,0:T(4,128)(2,1)} %param.14) | copy-start | bytes 393220
  8.7 49.3 %all-to-all-start = ((bf16[32,1,1]{2,1,0:T(2,128)(2,1)}), bf16[32,1,1]{2,1,0:T(2,128)(2,1)S(1)}, u32[]{:S(2)}, u32[]{:S(2)}) async-start(bf16[32,1,1]{2,1,0:T(2,128)(2,1)} %copy.40), calls=%async_computation | async-start | bytes 32768 | tf_op jit(solution)/shard_map/all_to_all | solution.py:74
  25.4 1.6 copy-start.10
  25.4 1.9 copy-start.6
  25.4 2.0 copy-start.9
  25.4 15.2 %copy-start.8 = (f32[896]{0:T(1024)S(1)}, f32[896]{0:T(1024)}, u32[]{:S(2)}) copy-start(f32[896]{0:T(1024)} %param.20) | copy-start | bytes 10756
  57.9 18.1 %all-to-all-start.3 = ((bf16[32,2,512]{2,1,0:T(2,128)(2,1)}), bf16[32,2,512]{2,1,0:T(2,128)(2,1)S(1)}, u32[]{:S(2)}, u32[]{:S(2)}) async-start(bf16[32,2,512]{2,1,0:T(2,128)(2,1)} %reshape.179), calls=%async_computation.3 | async-start | bytes 131072 | tf_op jit(solution)/shard_map/all_to_all | solution.py:71
  76.0 48.1 %all-to-all-start.5 = ((bf16[32,3,7168]{2,1,0:T(4,128)(2,1)}), bf16[32,3,7168]{2,1,0:T(4,128)(2,1)}, u32[]{:S(2)}, u32[]{:S(2)}) async-start(bf16[32,3,7168]{2,1,0:T(4,128)(2,1)} %reshape.169), calls=%async_computation.5 | async-start | bytes 3670016 | tf_op jit(solution)/shard_map/all_to_all | solution.py:150
  82.4 2.7 copy-start.2
  85.4 1.6 copy-start.4
  124.1 190.6 %all-to-all-start.2 = ((bf16[32,2,65536]{2,1,0:T(2,128)(2,1)}), bf16[32,2,65536]{2,1,0:T(2,128)(2,1)}, u32[]{:S(2)}, u32[]{:S(2)}) async-start(bf16[32,2,65536]{2,1,0:T(2,128)(2,1)} %reshape.181), calls=%async_computation.2 | async-start | bytes 16777216 | tf_op jit(solution)/shard_map/all_to_all | solution.py:70
  131.3 300.5 %reduce-scatter.2.cloned.1.call-start = ((), (), s32[]{:S(2)}) async-start(), calls=%async_computation.10 | async-start | bytes 3096576 | tf_op jit(solution)/shard_map/reduce_scatter | solution.py:26
  145.6 3.1 copy-start.3
  153.9 294.6 %all-gather.3.cloned.1.call-start = ((), (), s32[]{:S(2)}) async-start(), calls=%async_computation.8 | async-start | bytes 9437184 | tf_op jit(solution)/shard_map/all_gather | solution.py:97
  338.1 15.0 %copy-start.1 = (f32[4,256,512]{2,1,0:T(8,128)S(1)}, f32[4,256,512]{2,1,0:T(8,128)}, u32[]{:S(2)}) copy-start(f32[4,256,512]{2,1,0:T(8,128)} %mul.70) | copy-start | bytes 6291460
  358.4 38.0 %all-to-all-start.4 = ((bf16[32,2,8192]{2,1,0:T(2,128)(2,1)}), bf16[32,2,8192]{2,1,0:T(2,128)(2,1)S(1)}, u32[]{:S(2)}, u32[]{:S(2)}) async-start(bf16[32,2,8192]{2,1,0:T(2,128)(2,1)} %reshape.183), calls=%async_computation.4 | async-start | bytes 2097152 | tf_op jit(solution)/shard_map/all_to_all | solution.py:72
  371.5 82.7 %all-gather.5.cloned.1.call-start = ((), (), s32[]{:S(2)}) async-start(), calls=%async_computation.9 | async-start | bytes 1179648 | tf_op jit(solution)/shard_map/all_gather | solution.py:98
  371.5 28.2 %copy-start.12 = (s32[1,4]{1,0:T(1,128)S(1)}, s32[1,4]{1,0:T(1,128)}, u32[]{:S(2)}) copy-start(s32[1,4]{1,0:T(1,128)} %param.18) | copy-start | bytes 52
  371.6 37.9 %copy-start.11 = (f32[4,8]{1,0:T(4,128)S(1)}, f32[4,8]{1,0:T(4,128)}, u32[]{:S(2)}) copy-start(f32[4,8]{1,0:T(4,128)} %param.22) | copy-start | bytes 388
  371.6 38.2 %copy-start.7 = (bf16[4,1024]{1,0:T(4,128)(2,1)S(1)}, bf16[4,1024]{1,0:T(4,128)(2,1)}, u32[]{:S(2)}) copy-start(bf16[4,1024]{1,0:T(4,128)(2,1)} %param.16) | copy-start | bytes 24580
  397.4 51.1 %copy-start.5 = (bf16[4,16,512]{2,1,0:T(8,128)(2,1)S(1)}, bf16[4,16,512]{2,1,0:T(8,128)(2,1)}, u32[]{:S(2)}) copy-start(bf16[4,16,512]{2,1,0:T(8,128)(2,1)} %param.15) | copy-start | bytes 196612
  401.3 16.7 %all-to-all-start.1 = ((bf16[32,2,128]{2,1,0:T(2,128)(2,1)}), bf16[32,2,128]{2,1,0:T(2,128)(2,1)S(1)}, u32[]{:S(2)}, u32[]{:S(2)}) async-start(bf16[32,2,128]{2,1,0:T(2,128)(2,1)} %reshape.185), calls=%async_computation.1 | async-start | bytes 32768 | tf_op jit(solution)/shard_map/all_to_all | solution.py:73
  433.6 14.0 %all-to-all-start.6 = ((bf16[32,3,896]{2,1,0:T(4,128)(2,1)}), bf16[32,3,896]{2,1,0:T(4,128)(2,1)S(1)}, u32[]{:S(2)}, u32[]{:S(2)}) async-start(bf16[32,3,896]{2,1,0:T(4,128)(2,1)} %copy.48), calls=%async_computation.7 | async-start | bytes 458752 | tf_op jit(solution)/shard_map/all_to_all | solution.py:27
Sparse Core Ops, SparseCore 0:
  154.1 36.1 reduce-scatter.1
  354.9 55.6 all-gather.2
  412.6 26.1 all-gather.4
where the time goes:
time: 475 us; the launch traced here: 468 us
  waiting for transfers between devices  215 us (45%)
  starting transfers between devices  69.8 us (15%)
  local copies, waits for them, and re-layouts  59.5 us (13%)
  matrix products  44.1 us (9%)
  blocking collectives  41.7 us (9%)
  other arithmetic  23.2 us (5%)
  between operations  14.4 us (3%)
    all_to_all x1, waiting for transfers between devices, local(): lax.all_to_all(spread(packed), 'ctx', split_axis=0, concat_axis=0, tiled=...  156 us
    unnamed x36, local copies, waits for them, and re-layouts  40.9 us
    all_to_all x1, waiting for transfers between devices, local(): lax.all_to_all(spread(latent_rope), 'ctx', split_axis=0, concat_axis=0, t...  24.8 us
    dot_general x4, matrix products, own_rows(): jnp.dot(select, values, preferred_element_type=jnp.float32)  16.4 us
    all_gather x1, blocking collectives, local(): whole_rows = lax.all_gather(normed, 'expert', axis=1, tiled=True)  15.2 us
    all_gather x1, blocking collectives, local(): lax.all_gather(seen_own, 'expert', axis=1, tiled=True)  13.6 us
    all_to_all x1, starting transfers between devices, local(): lax.all_to_all(spread(latent_rope), 'ctx', split_axis=0, concat_axis=0, t...  13.1 us
    psum x1, blocking collectives, local(): squares = lax.psum(jnp.sum(stateful * stateful, axis=-1), 'expert')  12.9 us
  transfers between devices with their start and end apart: 10, of which 6 were waited for; matrix products, arithmetic and copies ran while one was open for 25% of the time, Pallas kernels for 0%

commit v1 on v0

v1 whole, which is shorter than its diff:
```python
import functools

import jax
import jax.numpy as jnp
from jax import lax
from jax.experimental import pallas as pl
from jax.experimental.pallas import tpu as pltpu
from jax.sharding import PartitionSpec as P

D = 7168
LAT = 512
ROPE = 64
BLK = 128
NX = 4
NZ = 8
NE = 8
NY = 4
REQ = 4
HD = 16
QW = 640
POS = 256
CAP = 3
SLOTS = NX * NZ * CAP
FEAT = D // NE
FF = 256

MESH = pl.DeviceIdType.MESH
BF = jnp.bfloat16
F32 = jnp.float32
score_scale = 192.0 ** (-0.5)
pack_limit = 448.0
HIDDEN_SCORE = -1e30


def coordinates():
    c = lax.axis_index("ctx")
    e = lax.axis_index("expert")
    return c, e, lax.div(c, NZ), lax.rem(c, NZ), lax.div(e, 2), lax.rem(e, 2)


def greet(peers):
    barrier = pltpu.get_barrier_semaphore()
    for peer in peers:
        pl.semaphore_signal(barrier, inc=1, device_id=peer, device_id_type=MESH)
    pl.semaphore_wait(barrier, len(peers))


def remote(src, dst, send_sem, recv_sem, peer):
    return pltpu.make_async_remote_copy(
        src_ref=src,
        dst_ref=dst,
        send_sem=send_sem,
        recv_sem=recv_sem,
        device_id=peer,
        device_id_type=MESH,
    )


class Ring:
    def __init__(self, buf, send, recv, x, z, e):
        self.buf, self.send, self.recv = buf, send, recv
        self.x, self.z, self.e = x, z, e
        self.copies = {}

    def step(self, s):
        for h in range(2):
            for way, sign in ((0, 1), (1, -1)):
                if s == 4 and h != way:
                    continue
                if s > 1:
                    self.copies[way, s - 1, h].wait_recv()
                origin = lax.rem(self.z + NZ - sign * (s - 1), NZ)
                block = self.buf.at[origin, pl.ds(2 * h, 2)]
                peer = (self.x * NZ + lax.rem(self.z + NZ + sign, NZ), self.e)
                n = (s - 1) * 4 + h * 2 + way
                copy = remote(block, block, self.send.at[n], self.recv.at[n], peer)
                copy.start()
                self.copies[way, s, h] = copy

    def finish(self):
        for way in range(2):
            self.copies[way, 3, 1 - way].wait_recv()
            self.copies[way, 4, way].wait_recv()
        for copy in self.copies.values():
            copy.wait_send()


def spread_kernel(
    q_ref, tok_ref, meta_ref, gain_ref,
    qz_ref, tk_ref, mt_ref, gn_ref,
    ring_s, ring_r, z_s, z_r, x_s, x_r, g_s, g_r,
):
    c, e, x, z, y, k = coordinates()

    def zp(d):
        return (x * NZ + lax.rem(z + d, NZ), e)

    def xp(d):
        return (lax.rem(x + d, NX) * NZ + z, e)

    def ep(d):
        return (c, lax.rem(e + d, NE))

    qz_ref[z] = q_ref[...]
    tk_ref[x, z] = tok_ref[...]
    mt_ref[x, z] = meta_ref[...]
    gn_ref[e] = gain_ref[...]
    greet([zp(d) for d in range(1, NZ)] + [xp(d) for d in range(1, NX)] + [ep(d) for d in range(1, NE)])
    z_copies = []
    for d in (1, 7, 2, 6, 3, 5, 4):
        z_copies.append(remote(meta_ref, mt_ref.at[x, z], z_s.at[0, d - 1], z_r.at[0, d - 1], zp(d)))
        z_copies.append(remote(tok_ref, tk_ref.at[x, z], z_s.at[1, d - 1], z_r.at[1, d - 1], zp(d)))
    for copy in z_copies:
        copy.start()
    ring = Ring(qz_ref, ring_s, ring_r, x, z, e)
    ring.step(1)
    gains = [remote(gain_ref, gn_ref.at[e], g_s.at[d - 1], g_r.at[d - 1], ep(d)) for d in range(1, NE)]
    for copy in gains:
        copy.start()
    ring.step(2)
    for copy in z_copies:
        copy.wait_recv()
    x_copies = []
    for d in range(1, NX):
        x_copies.append(remote(mt_ref.at[x], mt_ref.at[x], x_s.at[0, d - 1], x_r.at[0, d - 1], xp(d)))
        x_copies.append(remote(tk_ref.at[x], tk_ref.at[x], x_s.at[1, d - 1], x_r.at[1, d - 1], xp(d)))
    for copy in x_copies:
        copy.start()
    ring.step(3)
    ring.step(4)
    ring.finish()
    for copy in x_copies + gains:
        copy.wait_recv()
    for copy in z_copies + x_copies + gains:
        copy.wait_send()


def spread(q, tok, meta, gain):
    vmem = pl.BlockSpec(memory_space=pltpu.VMEM)
    dma = pltpu.SemaphoreType.DMA
    return pl.pallas_call(
        spread_kernel,
        out_shape=(
            jax.ShapeDtypeStruct((NZ,) + q.shape, q.dtype),
            jax.ShapeDtypeStruct((NX, NZ) + tok.shape, tok.dtype),
            jax.ShapeDtypeStruct((NX, NZ) + meta.shape, meta.dtype),
            jax.ShapeDtypeStruct((NE,) + gain.shape, gain.dtype),
        ),
        in_specs=[vmem] * 4,
        out_specs=(vmem,) * 4,
        scratch_shapes=[
            dma((16,)), dma((16,)),
            dma((2, 7)), dma((2, 7)),
            dma((2, 3)), dma((2, 3)),
            dma((7,)), dma((7,)),
        ],
        compiler_params=pltpu.CompilerParams(
            collective_id=0, has_side_effects=True, vmem_limit_bytes=16 * 1024 * 1024
        ),
    )(q, tok, meta, gain)


def layer_kernel(
    idx_ref, qz_ref, xt_ref, gain_ref, whi_ref, wlo_ref, rope_ref,
    lat_hbm, wg_hbm, wu_hbm, wd_hbm,
    att_ref, moe_ref,
    wg, wu, wd, lat, kcat, xbuf, xsend, qall, tall, xn, osend, orecv,
    ysib, ysr, yown, ysend, yrecv, xrs, xrr, zs, zr, og, oxs, oxr,
    w_sem, qx_s, qx_r, qy_s, qy_r, qk_s, qk_r, ty_s, ty_r, tk_s, tk_r,
    o_s, o_r, yk_s, yk_r, yy_s, yy_r, xr_s, xr_r, zr_s, zr_r, ring_s, ring_r, ox_s, ox_r,
):
    c, e, x, z, y, k = coordinates()

    def zp(d):
        return (x * NZ + lax.rem(z + d, NZ), e)

    def xp(d):
        return (lax.rem(x + d, NX) * NZ + z, e)

    def ep(d):
        return (c, lax.rem(e + d, NE))

    def yp(d):
        return (c, lax.rem(y + d, NY) * 2 + k)

    sib = (c, y * 2 + 1 - k)

    loads = [
        pltpu.make_async_copy(lat_hbm, lat, w_sem.at[0]),
        pltpu.make_async_copy(wg_hbm.at[0], wg, w_sem.at[1]),
        pltpu.make_async_copy(wu_hbm.at[0], wu, w_sem.at[2]),
        pltpu.make_async_copy(wd_hbm.at[0], wd, w_sem.at[3]),
    ]
    for load in loads:
        load.start()
    greet([zp(d) for d in range(1, NZ)] + [xp(d) for d in range(1, NX)] + [ep(d) for d in range(1, NE)])

    qx = []
    for d in range(1, NX):
        target = lax.rem(x + d, NX)
        for j in range(REQ):
            xsend[d - 1, j] = qz_ref[idx_ref[target * REQ + j]]
        qx.append(remote(xsend.at[d - 1], xbuf.at[x], qx_s.at[d - 1], qx_r.at[d - 1], xp(d)))
        qx[-1].start()
    for j in range(REQ):
        xbuf[x, j] = qz_ref[idx_ref[x * REQ + j]]

    ty = [remote(xt_ref, tall.at[e], ty_s.at[d - 1], ty_r.at[d - 1], yp(d)) for d in range(1, NY)]
    tk = [remote(xt_ref, tall.at[e], tk_s.at[0], tk_r.at[0], sib)]
    for copy in ty + tk:
        copy.start()
    tall[e] = xt_ref[...]

    for copy in qx:
        copy.wait_recv()
    for j in range(REQ):
        qall[j, e] = xbuf[idx_ref[16 + j], j]
    mine = qall.at[:, e]
    qy = [remote(mine, mine, qy_s.at[d - 1], qy_r.at[d - 1], yp(d)) for d in range(1, NY)]
    qk = [remote(mine, mine, qk_s.at[0], qk_r.at[0], sib)]
    for copy in qy + qk:
        copy.start()

    loads[0].wait()
    for j in range(REQ):
        for b in range(LAT // BLK):
            block = lat[j, :, b * BLK:(b + 1) * BLK].astype(F32)
            scale = ((jnp.max(jnp.abs(block), axis=-1, keepdims=True) + 1e-06) / pack_limit).astype(BF)
            scale = scale.astype(F32)
            packed = (block / scale).astype(BF)
            kcat[j, :, b * BLK:(b + 1) * BLK] = (packed.astype(F32) * scale).astype(BF)
        kcat[j, :, LAT:] = rope_ref[j]

    for d in range(1, NY):
        qy[d - 1].wait_recv()
        other = lax.rem(y + NY - d, NY) * 2 + k
        copy = remote(qall.at[:, other], qall.at[:, other], qk_s.at[d], qk_r.at[d], sib)
        copy.start()
        qk.append(copy)
    for d in range(1, NY):
        ty[d - 1].wait_recv()
        other = lax.rem(y + NY - d, NY) * 2 + k
        copy = remote(tall.at[other], tall.at[other], tk_s.at[d], tk_r.at[d], sib)
        copy.start()
        tk.append(copy)
    for copy in qk:
        copy.wait_recv()

    lanes = lax.broadcasted_iota(jnp.int32, (1, POS), 1) + e * POS
    side = lax.broadcasted_iota(jnp.int32, (HD * NE, QW - LAT), 1)
    for j in range(REQ):
        scores = lax.dot_general(
            qall[j].reshape(NE * HD, QW), kcat[j], (((1,), (1,)), ((), ())), preferred_element_type=F32
        )
        scores = jnp.where(lanes < idx_ref[20 + j], scores * score_scale, HIDDEN_SCORE)
        highest = jnp.max(scores, axis=-1, keepdims=True)
        weights = jnp.exp(scores - highest)
        total = jnp.sum(weights, axis=-1, keepdims=True)
        out = jnp.dot(weights.astype(BF), kcat[j, :, :LAT], preferred_element_type=F32) / total
        level = highest + jnp.log(total)
        first = level.astype(BF).astype(F32)
        second = (level - first).astype(BF).astype(F32)
        third = level - first - second
        tail = jnp.where(side == 0, first, jnp.where(side == 1, second, jnp.where(side == 2, third, 0.0)))
        osend[:, j, :, :LAT] = out.astype(BF).reshape(NE, HD, LAT)
        osend[:, j, :, LAT:] = tail.astype(BF).reshape(NE, HD, QW - LAT)
    oc = []
    for d in range(1, NE):
        copy = remote(osend.at[lax.rem(e + d, NE)], orecv.at[e], o_s.at[d - 1], o_r.at[d - 1], ep(d))
        copy.start()
        oc.append(copy)
    orecv[e] = osend[e]

    for copy in tk:
        copy.wait_recv()
    squares = jnp.zeros((SLOTS, 1), F32)
    for g in range(NE):
        rows = tall[g].astype(F32)
        squares = squares + jnp.sum(rows * rows, axis=-1, keepdims=True)
    inverse = lax.rsqrt(squares / D + 1e-06)
    for g in range(NE):
        xn[g] = (tall[g].astype(F32) * inverse * gain_ref[:, g * FEAT:(g + 1) * FEAT]).astype(BF)
    for load in loads[1:]:
        load.wait()
    gate = jnp.zeros((SLOTS, FF), F32)
    up = jnp.zeros((SLOTS, FF), F32)
    for g in range(NE):
        gate = gate + jnp.dot(xn[g], wg[g * FEAT:(g + 1) * FEAT, :], preferred_element_type=F32)
        up = up + jnp.dot(xn[g], wu[g * FEAT:(g + 1) * FEAT, :], preferred_element_type=F32)
    hidden = (jax.nn.silu(gate) * up).astype(BF)

    def project(target):
        columns = pl.ds(pl.multiple_of(target * FEAT, BLK), FEAT)
        return jnp.dot(hidden, wd[:, columns], preferred_element_type=F32)

    yk = []
    for d in range(NY):
        target = lax.rem(y + d + 1, NY) * 2 + 1 - k
        ysib[d] = project(target).astype(BF)
        copy = remote(ysib.at[d], ysr.at[d], yk_s.at[d], yk_r.at[d], sib)
        copy.start()
        yk.append(copy)
    for d in range(NY):
        yown[d] = project(lax.rem(y + d + 1, NY) * 2 + k)
    yy = []
    for d in range(NY - 1):
        yk[d].wait_recv()
        ysend[d] = (yown[d] + ysr[d].astype(F32)).astype(BF)
        copy = remote(ysend.at[d], yrecv.at[d], yy_s.at[d], yy_r.at[d], yp(d + 1))
        copy.start()
        yy.append(copy)

    for copy in oc:
        copy.wait_recv()
    for j in range(REQ):
        levels = [jnp.sum(orecv[g, j, :, LAT:].astype(F32), axis=-1, keepdims=True) for g in range(NE)]
        top = functools.reduce(jnp.maximum, levels)
        share = [jnp.exp(level - top) for level in levels]
        total = functools.reduce(jnp.add, share)
        acc = share[0] * orecv[0, j, :, :LAT].astype(F32)
        for g in range(1, NE):
            acc = acc + share[g] * orecv[g, j, :, :LAT].astype(F32)
        og[z, j] = (acc / total).astype(BF)
    ring = Ring(og, ring_s, ring_r, x, z, e)
    ring.step(1)

    yk[NY - 1].wait_recv()
    summed = yown[NY - 1] + ysr[NY - 1].astype(F32)
    for copy in yy:
        copy.wait_recv()
    for d in range(NY - 1):
        summed = summed + yrecv[d].astype(F32)
    rounded = summed.astype(BF)

    def weighted(target):
        rows = pl.ds(pl.multiple_of(target * 32, 32), 32)
        return jnp.dot(whi_ref[rows, :], rounded, preferred_element_type=F32) + jnp.dot(
            wlo_ref[rows, :], rounded, preferred_element_type=F32
        )

    xr = []
    for d in range(1, NX):
        xrs[d - 1] = weighted(lax.rem(x + d, NX)).astype(BF)
        copy = remote(xrs.at[d - 1], xrr.at[d - 1], xr_s.at[d - 1], xr_r.at[d - 1], xp(d))
        copy.start()
        xr.append(copy)
    own = weighted(x)
    ring.step(2)
    for copy in xr:
        copy.wait_recv()
    for d in range(NX - 1):
        own = own + xrr[d].astype(F32)
    for t in range(NZ):
        zs[t, 0:4, 0:512] = own[4 * t:4 * t + 4, 0:512]
        zs[t, 4:8, 0:384] = own[4 * t:4 * t + 4, 512:896]
        zs[t, 4:8, 384:512] = jnp.zeros((4, 128), F32)
    zc = []
    for d in range(1, NZ):
        copy = remote(zs.at[lax.rem(z + d, NZ)], zr.at[d - 1], zr_s.at[d - 1], zr_r.at[d - 1], zp(d))
        copy.start()
        zc.append(copy)
    ring.step(3)
    ring.step(4)
    for copy in zc:
        copy.wait_recv()
    final = zs[z]
    for d in range(NZ - 1):
        final = final + zr[d]
    moe_ref[:, 0:512] = final[0:4, :].astype(BF)
    moe_ref[:, 512:896] = final[4:8, 0:384].astype(BF)
    ring.finish()

    ox = []
    for d in range(1, NX):
        target = lax.rem(x + d, NX)
        for j in range(REQ):
            at = idx_ref[24 + target * REQ + j]
            oxs[d - 1, j] = og[at // REQ, at % REQ]
        ox.append(remote(oxs.at[d - 1], oxr.at[x], ox_s.at[d - 1], ox_r.at[d - 1], xp(d)))
        ox[-1].start()
    for j in range(REQ):
        at = idx_ref[24 + x * REQ + j]
        oxr[x, j] = og[at // REQ, at % REQ]
    for copy in ox:
        copy.wait_recv()
    for j in range(REQ):
        att_ref[j] = oxr[idx_ref[40 + j], j]
    for copy in qx + ty + tk + qy + qk + oc + yk + yy + xr + zc + ox:
        copy.wait_send()


def layer(idx, qz, xt, gain, whi, wlo, rope, lat, wg, wu, wd):
    vmem = pl.BlockSpec(memory_space=pltpu.VMEM)
    hbm = pl.BlockSpec(memory_space=pl.ANY)
    dma = pltpu.SemaphoreType.DMA
    V = pltpu.VMEM
    pairs = []
    for count in (3, 3, 4, 3, 4, 7, 4, 3, 3, 7, 16, 3):
        pairs += [dma((count,)), dma((count,))]
    return pl.pallas_call(
        layer_kernel,
        out_shape=(
            jax.ShapeDtypeStruct((REQ, HD, LAT), BF),
            jax.ShapeDtypeStruct((REQ, FEAT), BF),
        ),
        in_specs=[pl.BlockSpec(memory_space=pltpu.SMEM)] + [vmem] * 6 + [hbm] * 4,
        out_specs=(vmem, vmem),
        scratch_shapes=[
            V((D, FF), BF), V((D, FF), BF), V((FF, D), BF),
            V((REQ, POS, LAT), BF), V((REQ, POS, QW), BF),
            V((NX, REQ, HD, QW), BF), V((NX - 1, REQ, HD, QW), BF),
            V((REQ, NE, HD, QW), BF),
            V((NE, SLOTS, FEAT), BF), V((NE, SLOTS, FEAT), BF),
            V((NE, REQ, HD, QW), BF), V((NE, REQ, HD, QW), BF),
            V((NY, SLOTS, FEAT), BF), V((NY, SLOTS, FEAT), BF), V((NY, SLOTS, FEAT), F32),
            V((NY - 1, SLOTS, FEAT), BF), V((NY - 1, SLOTS, FEAT), BF),
            V((NX - 1, 32, FEAT), BF), V((NX - 1, 32, FEAT), BF),
            V((NZ, 8, 512), F32), V((NZ - 1, 8, 512), F32),
            V((NZ, REQ, HD, LAT), BF),
            V((NX - 1, REQ, HD, LAT), BF), V((NX, REQ, HD, LAT), BF),
            dma((4,)),
        ] + pairs,
        compiler_params=pltpu.CompilerParams(
            collective_id=1, has_side_effects=True, vmem_limit_bytes=48 * 1024 * 1024
        ),
    )(idx, qz, xt, gain, whi, wlo, rope, lat, wg, wu, wd)


def local(
    latent_plane,
    latent_rope,
    query_plane,
    query_rope,
    decode_hidden,
    lengths,
    owner,
    norm_gain,
    routes,
    combine,
    gate_weight,
    up_weight,
    down_weight,
):
    c, e, x, z, y, k = coordinates()
    experts = NX * NZ
    q = jnp.concatenate(
        [query_plane, query_rope.reshape(REQ, HD, ROPE), jnp.zeros((REQ, HD, QW - LAT - ROPE), BF)], axis=-1
    )
    tok = jnp.pad(decode_hidden, ((0, 0), (0, 128))).reshape(REQ, 4, 256).transpose(1, 0, 2).reshape(16, 256)
    named = routes[:, :, None] == jnp.arange(experts, dtype=jnp.int32)[None, None, :]
    dense = jnp.sum(jnp.where(named, combine[:, :, None], 0.0), axis=1)
    request = jnp.stack([owner[0], lengths[0]], axis=1).astype(F32)
    meta = jnp.concatenate(
        [jnp.pad(dense, ((0, 0), (0, 96))), jnp.pad(request, ((0, 0), (0, 126)))], axis=0
    )
    gain = jnp.pad(norm_gain.reshape(7, 128), ((0, 1), (0, 0)))
    rope = jnp.pad(latent_rope.reshape(REQ, POS, ROPE), ((0, 0), (0, 0), (0, QW - LAT - ROPE)))

    qz, tk, mt, gn = spread(q, tok, meta, gain)

    mt = mt.reshape(experts, 8, 128)
    gain_all = gn[:, :7].reshape(1, D)
    owners = mt[:, 4:, 0].astype(jnp.int32).reshape(experts * REQ)
    number = jnp.arange(experts * REQ, dtype=jnp.int32)
    rank = jnp.sum((owners[:, None] == owners[None, :]) & (number[None, :] < number[:, None]), axis=1).astype(jnp.int32)
    row = owners * REQ + rank
    request_of = jnp.sum(jnp.where(row[None, :] == number[:, None], number[None, :], 0), axis=1)
    here = ((number // REQ) % NZ) == z

    def at_z(values):
        return jnp.sum(jnp.where(here, values, 0).reshape(NX, NZ, REQ), axis=1).reshape(NX * REQ)

    def at_c(values):
        return lax.dynamic_slice(values, (c * REQ,), (REQ,))

    idx = jnp.concatenate(
        [
            at_z((owners % NZ) * REQ + rank),
            at_c(owners // NZ),
            lengths[0],
            at_z(((request_of // REQ) % NZ) * REQ + request_of % REQ),
            at_c(request_of // (REQ * NZ)),
        ]
    ).astype(jnp.int32)

    lane = jnp.arange(128, dtype=jnp.int32) == c
    share = jnp.sum(jnp.where(lane, mt[:, :4, :], 0.0), axis=-1)
    chosen = share > 0
    count = chosen.astype(jnp.int32)
    before = jnp.sum(
        jnp.where(jnp.arange(REQ)[None, :, None] > jnp.arange(REQ)[None, None, :], count[:, None, :], 0), axis=2
    )
    slot = (jnp.arange(experts, dtype=jnp.int32)[:, None] * CAP + before).reshape(experts * REQ)
    slot = jnp.where(chosen.reshape(-1), slot, -1)
    placing = jnp.arange(SLOTS, dtype=jnp.int32)[:, None] == slot[None, :]
    flat = share.reshape(-1)
    high = flat.astype(BF).astype(F32)
    back = jnp.arange(SLOTS, dtype=jnp.int32)[None, :] == slot[:, None]
    whi = jnp.where(back, high[:, None], 0.0).astype(BF)
    wlo = jnp.where(back, (flat - high)[:, None], 0.0).astype(BF)
    tokens = tk.reshape(experts, 4, REQ, 256).transpose(0, 2, 1, 3).reshape(experts * REQ, 1024)[:, :FEAT]
    xt = jnp.dot(placing.astype(BF), tokens, preferred_element_type=F32).astype(BF)

    att, moe = layer(
        idx, qz.reshape(NZ * REQ, HD, QW), xt, gain_all, whi, wlo, rope,
        latent_plane, gate_weight, up_weight, down_weight,
    )
    return att.reshape(REQ, HD * LAT), moe


def solution(mesh):
    placed = (
        P("ctx", "expert", None),
        P("ctx", "expert"),
        P("ctx", "expert", None),
        P("ctx", "expert"),
        P("ctx", "expert"),
        P("ctx", None),
        P("ctx", None),
        P("expert"),
        P("ctx", None),
        P("ctx", None),
        P("ctx", None, "expert"),
        P("ctx", None, "expert"),
        P("ctx", "expert", None),
    )
    return jax.shard_map(
        local,
        mesh=mesh,
        in_specs=placed,
        out_specs=(P("ctx", "expert"), P("ctx", "expert")),
        check_vma=False,
    )
```

time: 475 us -> 97.3 us (0.20); the launches traced: 468 us -> 96.4 us
  waiting for transfers between devices: 215 us -> 0 us
  Pallas kernels: 0 us -> 81.6 us
  starting transfers between devices: 69.8 us -> 0 us
  local copies, waits for them, and re-layouts: 59.5 us -> 11.1 us
  matrix products: 44.1 us -> 0.2 us
  blocking collectives: 41.7 us -> 0 us
  other arithmetic: 23.2 us -> 2.65 us
  between operations: 14.4 us -> 0.84 us
    all_to_all x7 -> x0, waiting for transfers between devices: 215 us -> none  [the longest x1 156 us: local(): lax.all_to_all(spread(packed), 'ctx', split_axis=0, concat_axis=0, tiled=...]
    pallas_call x0 -> x2, Pallas kernels: none -> 81.6 us  [the longest x1 58.5 us: layer(): pl.pallas_call(layer_kernel, out_shape=(jax.ShapeDtypeStruct((REQ, HD, LA...]
    all_to_all x7 -> x0, starting transfers between devices: 58.4 us -> none  [the longest x1 13.1 us: local(): lax.all_to_all(spread(latent_rope), 'ctx', split_axis=0, concat_axis=0, t...]
    dot_general x19 -> x1, matrix products: 44.1 us -> 0.2 us  [local(): jnp.dot(placing.astype(BF), tokens, preferred_element_type=F32).astype(BF)]
    unnamed x36 -> x8, local copies, waits for them, and re-layouts: 40.9 us -> 3.64 us
    all_gather x2 -> x0, blocking collectives: 28.8 us -> none  [the longest x1 15.2 us: local(): whole_rows = lax.all_gather(normed, 'expert', axis=1, tiled=True)]
    all_to_all x4 -> x0, other arithmetic: 14.2 us -> none  [the longest x1 11.5 us: local(): lax.all_to_all(spread(packed), 'ctx', split_axis=0, concat_axis=0, tiled=...]
    psum x1 -> x0, blocking collectives: 12.9 us -> none  [local(): squares = lax.psum(jnp.sum(stateful * stateful, axis=-1), 'expert')]
  transfers between devices with their start and end apart: 10 -> 0, of which waited for: 6 -> 0; matrix products, arithmetic and copies ran while one was open for 25% -> 0% of each run, Pallas kernels for 0% -> 0%
where the time goes in v1:
time: 97.3 us; the launch traced here: 96.4 us
  Pallas kernels  81.6 us (84%)
  local copies, waits for them, and re-layouts  11.1 us (11%)
  other arithmetic  2.65 us (3%)
    pallas_call x1, Pallas kernels, layer(): pl.pallas_call(layer_kernel, out_shape=(jax.ShapeDtypeStruct((REQ, HD, LA...  58.5 us
    pallas_call x1, Pallas kernels, spread(): pl.pallas_call(spread_kernel, out_shape=(jax.ShapeDtypeStruct((NZ,) + q.s...  23 us
    unnamed x8, local copies, waits for them, and re-layouts  3.64 us

profile of v1, /device:TPU:1, one launch (start us, length us, event | category | flops | bytes accessed | tf_op | source)
XLA Modules:
  0.0 96.4 jit_solution(9416603171237567850)
XLA Ops:
  0.6 0.0 copy-start.1
  0.6 0.9 reshape.159
  1.5 0.1 pad.31.clone
  1.6 0.9 maximum_maximum_fusion.q_ref
  2.5 0.7 pad.20
  3.2 0.7 copy.80
  3.9 0.7 copy.81
  4.7 0.1 add_convert_fusion
  4.7 0.8 select_reduce_fusion.1
  5.5 0.7 pad.23.gain_ref
  6.2 23.0 %shard_map.140 = (bf16[8,4,16,640]{3,2,1,0:T(8,128)(2,1)S(1)}, bf16[4,8,16,256]{3,2,1,0:T(8,128)(2,1)S(1)}, f32[4,8,8,128]{3,2,1,0:T(8,128)S(1)}, f32[8,8,128]{2,1,0:T(8,128)S(1)}) custom-call(bf16[4,16,640]{2,1,0:T(8,128)(2,1)S(1)} %maximum_maximum_fusion.q_ref, bf16[16,256]{1,0:T(8,128)(2,1)S(1)} %reshape.161.tok_ref, ...), custom_call_target="tpu_custom_call" | custom-call | tf_op jit(solution)/shard_map/pallas_call | solution.py:141
  29.3 0.3 copy.95
  29.6 0.1 convert_element_type.78
  29.7 0.2 convert_reduce_fusion
  29.9 0.1 select_reduce_fusion
  30.0 0.1 reduce_sum.74
  30.1 0.1 copy.86
  30.2 0.1 reduce_sum.71
  30.3 0.1 copy.84
  30.4 0.1 copy.94
  30.5 0.3 fusion.11
  30.8 0.1 copy.85
  30.9 0.1 reshape.164
  31.0 0.1 copy.90
  31.1 0.1 reshape.165
  31.2 0.1 dynamic_slice.7
  31.2 0.1 dynamic_slice.6
  31.3 0.7 concatenate.11.idx_ref
  32.0 0.1 fusion.1
  32.2 0.1 reduce_sum.77
  32.3 0.1 copy.91
  32.4 0.1 select_reduce_fusion.2
  32.5 0.1 copy.92
  32.6 0.1 add.117
  32.7 0.1 select_convert_fusion
  32.8 0.1 reshape.167
  32.9 0.1 copy.93
  33.0 0.2 convolution_convert_fusion.xt_ref
  33.3 1.2 %reshape.170 = bf16[4,256,64]{2,1,0:T(8,128)(2,1)S(1)} reshape(bf16[4,16384]{1,0:T(4,128)(2,1)} %param.14) | data formatting | bytes 262144 | tf_op jit(solution)/shard_map/reshape | solution.py:457
  34.4 0.1 pad.24.rope_ref
  34.5 0.0 copy-done.1
  34.5 0.0 copy-start
  34.5 2.0 %copy-done = bf16[1,7168,256]{2,1,0:T(8,128)(2,1)S(1)} copy-done((bf16[1,7168,256]{2,1,0:T(8,128)(2,1)S(1)}, bf16[1,7168,256]{2,1,0:T(8,128)(2,1)}, u32[]{:S(2)}) %copy-start) | copy-done | bytes 3670040
  36.6 58.5 %shard_map.141 = (bf16[4,16,512]{2,1,0:T(8,128)(2,1)S(1)}, bf16[4,896]{1,0:T(4,128)(2,1)S(1)}) custom-call(s32[44]{0:T(128)S(1)} %concatenate.11.idx_ref, bf16[32,16,640]{2,1,0:T(8,128)(2,1)S(1)} %bitcast.22, bf16[96,896]{1,0:T(8,128)(2,1)S(1)} %convolution_convert_fusion.xt_ref, f32[1,7168]{1,0:T(1,128)S(1)} %reshape.169.gain_ref, ...), custom_call_target="tpu_custom_call" | custom-call | tf_op jit(solution)/shard_map/pallas_call | solution.py:400
  95.1 0.7 copy.97
  95.8 0.6 copy.99
  (17 shorter events, 0.2 us)
Async XLA Ops:
  0.6 33.9 %copy-start.1 = (bf16[4,256,512]{2,1,0:T(8,128)(2,1)S(1)}, bf16[4,256,512]{2,1,0:T(8,128)(2,1)}, u32[]{:S(2)}) copy-start(bf16[4,256,512]{2,1,0:T(8,128)(2,1)} %lat_hbm.1) | copy-start | bytes 3145732
  34.5 2.0 %copy-start = (bf16[1,7168,256]{2,1,0:T(8,128)(2,1)S(1)}, bf16[1,7168,256]{2,1,0:T(8,128)(2,1)}, u32[]{:S(2)}) copy-start(bf16[1,7168,256]{2,1,0:T(8,128)(2,1)} %wg_hbm.1) | copy-start | bytes 11010052

commit v2 on v1

v2 whole, which is shorter than its diff:
```python
import functools

import jax
import jax.numpy as jnp
from jax import lax
from jax.experimental import pallas as pl
from jax.experimental.pallas import tpu as pltpu
from jax.sharding import PartitionSpec as P

D = 7168
LAT = 512
ROPE = 64
BLK = 128
NX = 4
NZ = 8
NE = 8
NY = 4
REQ = 4
HD = 16
QW = 640
POS = 256
CAP = 3
SLOTS = NX * NZ * CAP
FEAT = D // NE
FF = 256

MESH = pl.DeviceIdType.MESH
BF = jnp.bfloat16
F32 = jnp.float32
score_scale = 192.0 ** (-0.5)
pack_limit = 448.0
HIDDEN_SCORE = -1e30


def coordinates():
    c = lax.axis_index("ctx")
    e = lax.axis_index("expert")
    return c, e, lax.div(c, NZ), lax.rem(c, NZ), lax.div(e, 2), lax.rem(e, 2)


def greet(peers):
    barrier = pltpu.get_barrier_semaphore()
    for peer in peers:
        pl.semaphore_signal(barrier, inc=1, device_id=peer, device_id_type=MESH)
    return lambda: pl.semaphore_wait(barrier, len(peers))


def remote(src, dst, send_sem, recv_sem, peer):
    return pltpu.make_async_remote_copy(
        src_ref=src,
        dst_ref=dst,
        send_sem=send_sem,
        recv_sem=recv_sem,
        device_id=peer,
        device_id_type=MESH,
    )


class Gather:
    def __init__(self, buf, send, recv, x, z, e):
        self.buf, self.send, self.recv = buf, send, recv
        self.x, self.z, self.e = x, z, e
        self.copies = {}

    def put(self, origin, hop, sign, low):
        block = self.buf.at[lax.rem(self.z + 2 * NZ - sign * origin, NZ), pl.ds(low, 2)]
        peer = (self.x * NZ + lax.rem(self.z + 2 * NZ + sign * hop, NZ), self.e)
        n = len(self.copies)
        copy = remote(block, block, self.send.at[n], self.recv.at[n], peer)
        copy.start()
        self.copies[origin + hop, sign, low] = copy

    def start(self):
        for hop in (2, 1):
            for low in (0, 2):
                for sign in (1, -1):
                    self.put(0, hop, sign, low)

    def forward(self):
        for first in (True, False):
            for sign in (1, -1):
                low = 0 if first == (sign == 1) else 2
                self.copies[2, sign, low].wait_recv()
                if first:
                    self.put(2, 2, sign, low)
                self.put(2, 1, sign, low)

    def finish(self):
        for (distance, sign, low), copy in self.copies.items():
            if distance != 2:
                copy.wait_recv()

    def drain(self):
        for copy in self.copies.values():
            copy.wait_send()


def three_parts(level, side):
    first = level.astype(BF).astype(F32)
    second = (level - first).astype(BF).astype(F32)
    third = level - first - second
    return jnp.where(side == 0, first, jnp.where(side == 1, second, jnp.where(side == 2, third, 0.0))).astype(BF)


def merge(parts):
    levels = [jnp.sum(part[:, LAT:].astype(F32), axis=-1, keepdims=True) for part in parts]
    top = functools.reduce(jnp.maximum, levels)
    share = [jnp.exp(level - top) for level in levels]
    total = functools.reduce(jnp.add, share)
    acc = share[0] * parts[0][:, :LAT].astype(F32)
    for weight, part in zip(share[1:], parts[1:]):
        acc = acc + weight * part[:, :LAT].astype(F32)
    return acc / total, top + jnp.log(total)


def bits(number, shift, count):
    return jnp.bitwise_and(jnp.right_shift(number, shift), count - 1)


def iota(shape, axis):
    return lax.broadcasted_iota(jnp.int32, shape, axis)


def layer_kernel(
    owner_ref, length_ref, routes_ref, combine_ref,
    q_ref, qr_ref, tok_ref, gain_ref, rope_ref,
    lat_hbm, wg_hbm, wu_hbm, wd_hbm,
    att_ref, moe_ref,
    table, wg, wu, wd, lat, kcat, qz, xbuf, xsend, qall, xt, tall, xn, opart, osib, omine, oin,
    ysib, ysr, yown, ysend, yrecv, tw, xrs, xrr, zs, zr, og, oxs, oxr, af,
    tokf, tokb, tk, gall, mzs, mzr, mxs, mxr, mrow, owz, owx, tbl, phi, plo,
    w_sem, t_sem, mz_s, mz_r, oz_s, oz_r, kz_s, kz_r, mx_s, mx_r, wx_s, wx_r, kx_s, kx_r, g_s, g_r,
    qz_s, qz_r, qx_s, qx_r, qy_s, qy_r, qk_s, qk_r, ty_s, ty_r, tk_s, tk_r,
    os_s, os_r, o_s, o_r, yk_s, yk_r, yy_s, yy_r, xr_s, xr_r, zr_s, zr_r, og_s, og_r, ox_s, ox_r,
):
    c, e, x, z, y, k = coordinates()
    pending = []

    def zp(d):
        return (x * NZ + lax.rem(z + d, NZ), e)

    def xp(d):
        return (lax.rem(x + d, NX) * NZ + z, e)

    def ep(d):
        return (c, lax.rem(e + d, NE))

    def yp(d):
        return (c, lax.rem(y + d, NY) * 2 + k)

    sib = (c, y * 2 + 1 - k)

    def start(src, dst, send_sem, recv_sem, peer):
        copy = remote(src, dst, send_sem, recv_sem, peer)
        copy.start()
        pending.append(copy)
        return copy

    loads = [
        pltpu.make_async_copy(lat_hbm, lat, w_sem.at[0]),
        pltpu.make_async_copy(wg_hbm.at[0], wg, w_sem.at[1]),
        pltpu.make_async_copy(wu_hbm.at[0], wu, w_sem.at[2]),
        pltpu.make_async_copy(wd_hbm.at[0], wd, w_sem.at[3]),
    ]
    loads[0].start()
    wait_for_all = greet(
        [zp(d) for d in range(1, NZ)] + [xp(d) for d in range(1, NX)] + [ep(d) for d in range(1, NE)]
    )
    for load in loads[1:]:
        load.start()

    lane = iota((8, 128), 1)
    mine = jnp.zeros((8, 128), jnp.int32)
    for j in range(REQ):
        mine = jnp.where(lane == c * REQ + j, owner_ref[0, j], mine)
    owz[z] = mine
    row = iota((64, 128), 0)
    expert = jnp.bitwise_and(row, 7) * NZ + jnp.right_shift(row, 3)
    wide = iota((64, 128), 1)
    weights = jnp.zeros((64, 128), F32)
    for j in range(REQ):
        for n in range(8):
            hit = (expert == routes_ref[j, n]) & (wide == c * REQ + j)
            weights = jnp.where(hit, combine_ref[j, n], weights)
    mzs[...] = weights.reshape(8, 8, 128)
    state = tok_ref[...].astype(F32)
    for g in range(4):
        width = 256 if g < 3 else 128
        tokf[4 * g:4 * g + 4, 0:width] = state[:, g * 256:g * 256 + width]
    tokf[12:16, 128:256] = jnp.zeros((4, 128), F32)
    tokb[...] = tokf[...].astype(BF)
    gall[e] = gain_ref[...]
    qz[z, :, :, 0:LAT] = q_ref[...]
    turned = jnp.concatenate(
        [
            jnp.where(
                jnp.right_shift(iota((HD, HD * ROPE), 1), 6) == iota((HD, HD * ROPE), 0),
                jnp.broadcast_to(qr_ref[...].astype(F32)[j:j + 1, :], (HD, HD * ROPE)),
                0.0,
            )
            for j in range(REQ)
        ],
        axis=0,
    ).astype(BF)
    fold = (jnp.bitwise_and(iota((HD * ROPE, 128), 0), 63) == iota((HD * ROPE, 128), 1)).astype(F32).astype(BF)
    qz[z, :, :, LAT:] = jnp.dot(turned, fold, preferred_element_type=F32).astype(BF).reshape(REQ, HD, 128)

    wait_for_all()
    around = (1, 7, 2, 6, 3, 5, 4)
    oz = [start(owz.at[z], owz.at[z], oz_s.at[d - 1], oz_r.at[d - 1], zp(d)) for d in around]
    mz = [
        start(mzs.at[lax.rem(z + d, NZ)], mzr.at[z], mz_s.at[d - 1], mz_r.at[d - 1], zp(d)) for d in around
    ]
    kz = [start(tokb, tk.at[x, z], kz_s.at[d - 1], kz_r.at[d - 1], zp(d)) for d in around]
    gather = Gather(qz, qz_s, qz_r, x, z, e)
    gather.start()
    gains = [start(gain_ref, gall.at[e], g_s.at[d - 1], g_r.at[d - 1], ep(d)) for d in range(1, NE)]
    mzr[z] = mzs[z]
    tk[x, z] = tokb[...]

    loads[0].wait()
    for j in range(REQ):
        for b in range(LAT // BLK):
            block = lat[j, :, b * BLK:(b + 1) * BLK].astype(F32)
            scale = ((jnp.max(jnp.abs(block), axis=-1, keepdims=True) + 1e-06) / pack_limit).astype(BF)
            scale = scale.astype(F32)
            packed = (block / scale).astype(BF)
            kcat[j, :, b * BLK:(b + 1) * BLK] = (packed.astype(F32) * scale).astype(BF)
        kcat[j, :, LAT:] = rope_ref[j]

    for copy in oz + mz:
        copy.wait_recv()
    owx[x] = functools.reduce(jnp.add, [owz[d] for d in range(NZ)])
    mxs[...] = functools.reduce(jnp.add, [mzr[d] for d in range(NZ)])
    mxr[x] = mxs[...]
    wx = [start(owx.at[x], owx.at[x], wx_s.at[d - 1], wx_r.at[d - 1], xp(d)) for d in range(1, NX)]
    mx = [start(mxs, mxr.at[x], mx_s.at[d - 1], mx_r.at[d - 1], xp(d)) for d in range(1, NX)]
    for copy in kz:
        copy.wait_recv()
    kx = [start(tk.at[x], tk.at[x], kx_s.at[d - 1], kx_r.at[d - 1], xp(d)) for d in range(1, NX)]
    gather.forward()

    for copy in wx + mx:
        copy.wait_recv()
    sub = iota((128, 128), 0)
    col = iota((128, 128), 1)
    owners = functools.reduce(jnp.add, [owx[d] for d in range(NX)])[0:1, :]
    across = jnp.broadcast_to(owners, (128, 128))
    rank = jnp.sum(jnp.where((across.T == across) & (sub < col), 1, 0), axis=0, keepdims=True)
    place = jnp.broadcast_to(owners * REQ + rank, (128, 128)).T
    request_of = jnp.sum(jnp.where(place == col, sub, 0), axis=0, keepdims=True)
    eight = iota((8, 128), 0)
    tbl[...] = jnp.where(eight == 0, owners, jnp.where(eight == 1, rank, request_of))
    to_scalars = pltpu.make_async_copy(tbl, table, t_sem.at[0])
    to_scalars.start()

    mrow[...] = functools.reduce(jnp.add, [mxr[d] for d in range(NX)])
    share = mrow[pl.ds(x, 1), :]
    chosen = jnp.where(share > 0, 1.0, 0.0)
    earlier = ((jnp.right_shift(sub, 2) == jnp.right_shift(col, 2)) & (sub < col)).astype(F32).astype(BF)
    before = jnp.dot(jnp.broadcast_to(chosen, (8, 128)).astype(BF), earlier, preferred_element_type=F32)[0:1, :]
    slot = (jnp.right_shift(iota((1, 128), 1), 2) * CAP).astype(F32) + before
    placing = jnp.where(iota((SLOTS, 128), 0).astype(F32) == slot, chosen, 0.0)
    scaled = placing * share
    high = scaled.astype(BF)
    phi[...] = high
    plo[...] = (scaled - high.astype(F32)).astype(BF)
    token_of = iota((128, 512), 1)
    token_of = jnp.right_shift(token_of, 4) * REQ + jnp.bitwise_and(token_of, 3)
    widen = (token_of == iota((128, 512), 0)).astype(F32).astype(BF)
    placing = jnp.dot(placing.astype(BF), widen, preferred_element_type=F32)
    group = jnp.bitwise_and(jnp.right_shift(iota((SLOTS, 512), 1), 2), 3)
    for copy in kx:
        copy.wait_recv()
    states = tk[...].reshape(512, 256)
    for g in range(4):
        width = 256 if g < 3 else 128
        part = jnp.where(group == g, placing, 0.0).astype(BF)
        xt[:, g * 256:g * 256 + width] = jnp.dot(
            part, states[:, 0:width], preferred_element_type=F32
        ).astype(BF)

    ty = [start(xt, tall.at[e], ty_s.at[d - 1], ty_r.at[d - 1], yp(d)) for d in range(1, NY)]
    tc = [start(xt, tall.at[e], tk_s.at[0], tk_r.at[0], sib)]
    tall[e] = xt[...]

    gather.finish()
    to_scalars.wait()
    qx = []
    for d in range(1, NX):
        target = lax.rem(x + d, NX)
        for j in range(REQ):
            r = (target * NZ + z) * REQ + j
            xsend[d - 1, j] = qz[bits(table[0, r], 0, NZ), bits(table[1, r], 0, REQ)]
        qx.append(start(xsend.at[d - 1], xbuf.at[x], qx_s.at[d - 1], qx_r.at[d - 1], xp(d)))
    for j in range(REQ):
        r = c * REQ + j
        xbuf[x, j] = qz[bits(table[0, r], 0, NZ), bits(table[1, r], 0, REQ)]

    for copy in qx:
        copy.wait_recv()
    for j in range(REQ):
        qall[j, e] = xbuf[bits(table[0, c * REQ + j], 3, NX), j]
    own = qall.at[:, e]
    qy = [start(own, own, qy_s.at[d - 1], qy_r.at[d - 1], yp(d)) for d in range(1, NY)]
    qk = [start(own, own, qk_s.at[0], qk_r.at[0], sib)]
    for d in range(1, NY):
        ty[d - 1].wait_recv()
        other = lax.rem(y + NY - d, NY) * 2 + k
        tc.append(start(tall.at[other], tall.at[other], tk_s.at[d], tk_r.at[d], sib))
    for d in range(1, NY):
        qy[d - 1].wait_recv()
        other = lax.rem(y + NY - d, NY) * 2 + k
        block = qall.at[:, other]
        qk.append(start(block, block, qk_s.at[d], qk_r.at[d], sib))
    for copy in qk:
        copy.wait_recv()

    lanes = iota((1, POS), 1) + e * POS
    side = iota((HD * NE, QW - LAT), 1)
    oc = []
    for j in range(REQ):
        scores = lax.dot_general(
            qall[j].reshape(NE * HD, QW), kcat[j], (((1,), (1,)), ((), ())), preferred_element_type=F32
        )
        scores = jnp.where(lanes < length_ref[0, j], scores * score_scale, HIDDEN_SCORE)
        highest = jnp.max(scores, axis=-1, keepdims=True)
        likely = jnp.exp(scores - highest)
        total = jnp.sum(likely, axis=-1, keepdims=True)
        out = jnp.dot(likely.astype(BF), kcat[j, :, :LAT], preferred_element_type=F32) / total
        tail = three_parts(highest + jnp.log(total), side)
        out = out.astype(BF).reshape(NY, 2, HD, LAT)
        tail = tail.reshape(NY, 2, HD, QW - LAT)
        for core in range(2):
            opart[core, j, :, :, :LAT] = out[:, core]
            opart[core, j, :, :, LAT:] = tail[:, core]
        oc.append(start(opart.at[1 - k, j], osib.at[j], os_s.at[j], os_r.at[j], sib))

    for copy in tc + gains:
        copy.wait_recv()
    squares = jnp.zeros((SLOTS, 1), F32)
    for g in range(NE):
        rows = tall[g].astype(F32)
        squares = squares + jnp.sum(rows * rows, axis=-1, keepdims=True)
    inverse = lax.rsqrt(squares / D + 1e-06)
    for g in range(NE):
        for b in range(FEAT // 128):
            part = tall[g, :, b * 128:(b + 1) * 128].astype(F32)
            xn[g, :, b * 128:(b + 1) * 128] = (part * inverse * gall[g, b:b + 1, :]).astype(BF)

    side = iota((NY * HD, QW - LAT), 1)
    for j in range(REQ):
        oc[j].wait_recv()
        values, level = merge([opart[k, j].reshape(NY * HD, QW), osib[j].reshape(NY * HD, QW)])
        omine[:, j, :, :LAT] = values.astype(BF).reshape(NY, HD, LAT)
        omine[:, j, :, LAT:] = three_parts(level, side).reshape(NY, HD, QW - LAT)
    oy = [
        start(omine.at[lax.rem(y + d, NY)], oin.at[d - 1], o_s.at[d - 1], o_r.at[d - 1], yp(d))
        for d in range(1, NY)
    ]

    for load in loads[1:]:
        load.wait()
    gate = jnp.zeros((SLOTS, FF), F32)
    up = jnp.zeros((SLOTS, FF), F32)
    for g in range(NE):
        gate = gate + jnp.dot(xn[g], wg[g * FEAT:(g + 1) * FEAT, :], preferred_element_type=F32)
        up = up + jnp.dot(xn[g], wu[g * FEAT:(g + 1) * FEAT, :], preferred_element_type=F32)
    hidden = (jax.nn.silu(gate) * up).astype(BF)

    def project(target):
        columns = pl.ds(pl.multiple_of(target * FEAT, BLK), FEAT)
        return jnp.dot(hidden, wd[:, columns], preferred_element_type=F32)

    yk = []
    for d in range(NY):
        ysib[d] = project(lax.rem(y + d + 1, NY) * 2 + 1 - k).astype(BF)
        yk.append(start(ysib.at[d], ysr.at[d], yk_s.at[d], yk_r.at[d], sib))
    yy = []
    for d in range(NY):
        yown[d] = project(lax.rem(y + d + 1, NY) * 2 + k)
    for d in range(NY - 1):
        yk[d].wait_recv()
        ysend[d] = (yown[d] + ysr[d].astype(F32)).astype(BF)
        yy.append(start(ysend.at[d], yrecv.at[d], yy_s.at[d], yy_r.at[d], yp(d + 1)))

    for copy in oy:
        copy.wait_recv()
    for j in range(REQ):
        values, level = merge([omine[y, j]] + [oin[d, j] for d in range(NY - 1)])
        og[z, j] = values.astype(BF)
    back = Gather(og, og_s, og_r, x, z, e)
    back.start()

    yk[NY - 1].wait_recv()
    summed = yown[NY - 1] + ysr[NY - 1].astype(F32)
    back.forward()
    for copy in yy:
        copy.wait_recv()
    for d in range(NY - 1):
        summed = summed + yrecv[d].astype(F32)
    rounded = summed.astype(BF)
    first_rows = (((0,), (0,)), ((), ()))
    both = lax.dot_general(phi[...], rounded, first_rows, preferred_element_type=F32)
    both = both + lax.dot_general(plo[...], rounded, first_rows, preferred_element_type=F32)
    tw[...] = both.reshape(NX, 32, FEAT)
    xr = []
    for d in range(1, NX):
        xrs[d - 1] = tw[lax.rem(x + d, NX)].astype(BF)
        xr.append(start(xrs.at[d - 1], xrr.at[d - 1], xr_s.at[d - 1], xr_r.at[d - 1], xp(d)))
    for copy in xr:
        copy.wait_recv()
    own = tw[x]
    for d in range(NX - 1):
        own = own + xrr[d].astype(F32)
    for t in range(NZ):
        zs[t, 0:4, 0:512] = own[4 * t:4 * t + 4, 0:512]
        zs[t, 4:8, 0:384] = own[4 * t:4 * t + 4, 512:896]
        zs[t, 4:8, 384:512] = jnp.zeros((4, 128), F32)
    zc = [
        start(zs.at[lax.rem(z + d, NZ)], zr.at[d - 1], zr_s.at[d - 1], zr_r.at[d - 1], zp(d)) for d in around
    ]

    back.finish()
    ox = []
    for d in range(1, NX):
        target = lax.rem(x + d, NX)
        for j in range(REQ):
            r = table[2, (target * NZ + z) * REQ + j]
            oxs[d - 1, j] = og[bits(r, 2, NZ), bits(r, 0, REQ)]
        ox.append(start(oxs.at[d - 1], oxr.at[x], ox_s.at[d - 1], ox_r.at[d - 1], xp(d)))
    for j in range(REQ):
        r = table[2, c * REQ + j]
        oxr[x, j] = og[bits(r, 2, NZ), bits(r, 0, REQ)]

    for copy in zc:
        copy.wait_recv()
    final = zs[z]
    for d in range(NZ - 1):
        final = final + zr[d]
    moe_ref[:, 0:512] = final[0:4, :].astype(BF)
    moe_ref[:, 512:896] = final[4:8, 0:384].astype(BF)

    for copy in ox:
        copy.wait_recv()
    for j in range(REQ):
        values = oxr[bits(table[2, c * REQ + j], 5, NX), j].astype(F32)
        for h in range(HD):
            af[j:j + 1, h * LAT:(h + 1) * LAT] = values[h:h + 1, :]
    att_ref[...] = af[...].astype(BF)
    for copy in pending:
        copy.wait_send()
    gather.drain()
    back.drain()


def layer(owner, lengths, routes, combine, q, qr, tok, gain, rope, lat, wg, wu, wd):
    vmem = pl.BlockSpec(memory_space=pltpu.VMEM)
    smem = pl.BlockSpec(memory_space=pltpu.SMEM)
    hbm = pl.BlockSpec(memory_space=pl.ANY)
    dma = pltpu.SemaphoreType.DMA
    V = pltpu.VMEM
    pairs = []
    for count in (7, 7, 7, 3, 3, 3, 7, 14, 3, 3, 4, 3, 4, 4, 3, 4, 3, 3, 7, 14, 3):
        pairs += [dma((count,)), dma((count,))]
    return pl.pallas_call(
        layer_kernel,
        out_shape=(
            jax.ShapeDtypeStruct((REQ, HD * LAT), BF),
            jax.ShapeDtypeStruct((REQ, FEAT), BF),
        ),
        in_specs=[smem] * 4 + [vmem] * 5 + [hbm] * 4,
        out_specs=(vmem, vmem),
        scratch_shapes=[
            pltpu.SMEM((8, 128), jnp.int32),
            V((D, FF), BF), V((D, FF), BF), V((FF, D), BF),
            V((REQ, POS, LAT), BF), V((REQ, POS, QW), BF),
            V((NZ, REQ, HD, QW), BF),
            V((NX, REQ, HD, QW), BF), V((NX - 1, REQ, HD, QW), BF),
            V((REQ, NE, HD, QW), BF),
            V((SLOTS, FEAT), BF), V((NE, SLOTS, FEAT), BF), V((NE, SLOTS, FEAT), BF),
            V((2, REQ, NY, HD, QW), BF), V((REQ, NY, HD, QW), BF),
            V((NY, REQ, HD, QW), BF), V((NY - 1, REQ, HD, QW), BF),
            V((NY, SLOTS, FEAT), BF), V((NY, SLOTS, FEAT), BF), V((NY, SLOTS, FEAT), F32),
            V((NY - 1, SLOTS, FEAT), BF), V((NY - 1, SLOTS, FEAT), BF),
            V((NX, 32, FEAT), F32),
            V((NX - 1, 32, FEAT), BF), V((NX - 1, 32, FEAT), BF),
            V((NZ, 8, 512), F32), V((NZ - 1, 8, 512), F32),
            V((NZ, REQ, HD, LAT), BF),
            V((NX - 1, REQ, HD, LAT), BF), V((NX, REQ, HD, LAT), BF),
            V((REQ, HD * LAT), F32),
            V((16, 256), F32), V((16, 256), BF), V((NX, NZ, 16, 256), BF),
            V((NE, 7, 128), F32),
            V((NZ, 8, 128), F32), V((NZ, 8, 128), F32),
            V((8, 128), F32), V((NX, 8, 128), F32), V((8, 128), F32),
            V((NZ, 8, 128), jnp.int32), V((NX, 8, 128), jnp.int32), V((8, 128), jnp.int32),
            V((SLOTS, 128), BF), V((SLOTS, 128), BF),
            dma((4,)), dma((1,)),
        ] + pairs,
        compiler_params=pltpu.CompilerParams(
            collective_id=0, has_side_effects=True, vmem_limit_bytes=48 * 1024 * 1024
        ),
    )(owner, lengths, routes, combine, q, qr, tok, gain, rope, lat, wg, wu, wd)


def local(
    latent_plane,
    latent_rope,
    query_plane,
    query_rope,
    decode_hidden,
    lengths,
    owner,
    norm_gain,
    routes,
    combine,
    gate_weight,
    up_weight,
    down_weight,
):
    rope = jnp.pad(latent_rope.reshape(REQ, POS, ROPE), ((0, 0), (0, 0), (0, QW - LAT - ROPE)))
    return layer(
        owner, lengths, routes, combine, query_plane, query_rope, decode_hidden,
        norm_gain.reshape(7, 128), rope, latent_plane, gate_weight, up_weight, down_weight,
    )


def solution(mesh):
    placed = (
        P("ctx", "expert", None),
        P("ctx", "expert"),
        P("ctx", "expert", None),
        P("ctx", "expert"),
        P("ctx", "expert"),
        P("ctx", None),
        P("ctx", None),
        P("expert"),
        P("ctx", None),
        P("ctx", None),
        P("ctx", None, "expert"),
        P("ctx", None, "expert"),
        P("ctx", "expert", None),
    )
    return jax.shard_map(
        local,
        mesh=mesh,
        in_specs=placed,
        out_specs=(P("ctx", "expert"), P("ctx", "expert")),
        check_vma=False,
    )
```

time: 97.3 us -> 77 us (0.79)
  Pallas kernels: 81.6 us -> 64.7 us
  other arithmetic: 2.65 us -> 0 us
    pallas_call x2 -> x1, Pallas kernels: 81.6 us -> 64.7 us  [layer(): pl.pallas_call(layer_kernel, out_shape=(jax.ShapeDtypeStruct((REQ, HD * L...]
    unnamed x8 -> x22, local copies, waits for them, and re-layouts: 3.64 us -> 10.1 us
    reduce_sum x6 -> x0, other arithmetic: 1.52 us -> none  [the longest x1 0.78 us: local(): dense = jnp.sum(jnp.where(named, combine[:, :, None], 0.0), axis=1)]
    another operation x2 -> x0, local copies, waits for them, and re-layouts: 1.48 us -> none  [local(): request = jnp.stack([owner[0], lengths[0]], axis=1).astype(F32)]
    pad x2 -> x0, local copies, waits for them, and re-layouts: 1.4 us -> none  [the longest x1 0.7 us: local(): jnp.pad(decode_hidden, ((0, 0), (0, 128))).reshape(REQ, 4, 256)]
    reshape x7 -> x0, local copies, waits for them, and re-layouts: 1.25 us -> none  [the longest x1 0.87 us: local(): query_rope.reshape(REQ, HD, ROPE)]
where the time goes in v2:
time: 77 us; the launch traced here: 76.6 us
  Pallas kernels  64.7 us (84%)
  local copies, waits for them, and re-layouts  11.3 us (15%)
    pallas_call x1, Pallas kernels, layer(): pl.pallas_call(layer_kernel, out_shape=(jax.ShapeDtypeStruct((REQ, HD * L...  64.7 us
    unnamed x22, local copies, waits for them, and re-layouts  10.1 us

profile of v2, /device:TPU:1, one launch (start us, length us, event | category | flops | bytes accessed | tf_op | source)
XLA Modules:
  0.0 76.6 jit_solution(349719393181740008)
XLA Ops:
  0.6 1.2 %reshape.11 = bf16[4,256,64]{2,1,0:T(8,128)(2,1)S(1)} reshape(bf16[4,16384]{1,0:T(4,128)(2,1)} %param.14) | data formatting | bytes 262144 | tf_op jit(solution)/shard_map/reshape | solution.py:521
  1.8 0.1 pad.4.rope_ref
  1.9 0.0 copy-start
  1.9 2.0 %copy-done = bf16[1,7168,256]{2,1,0:T(8,128)(2,1)S(1)} copy-done((bf16[1,7168,256]{2,1,0:T(8,128)(2,1)S(1)}, bf16[1,7168,256]{2,1,0:T(8,128)(2,1)}, u32[]{:S(2)}) %copy-start) | copy-done | bytes 3670040
  3.9 0.0 copy-start.1
  3.9 1.2 %copy-done.1 = bf16[4,256,512]{2,1,0:T(8,128)(2,1)S(1)} copy-done((bf16[4,256,512]{2,1,0:T(8,128)(2,1)S(1)}, bf16[4,256,512]{2,1,0:T(8,128)(2,1)}, u32[]{:S(2)}) %copy-start.1) | copy-done | bytes 1048600
  5.1 0.0 copy-start.2
  5.1 0.8 %copy-done.2 = bf16[4,16,512]{2,1,0:T(8,128)(2,1)S(1)} copy-done((bf16[4,16,512]{2,1,0:T(8,128)(2,1)S(1)}, bf16[4,16,512]{2,1,0:T(8,128)(2,1)}, u32[]{:S(2)}) %copy-start.2) | copy-done | bytes 65560
  6.0 0.0 copy-start.3
  6.0 0.7 copy-done.3
  6.7 0.0 copy-start.4
  6.7 0.7 copy-done.4
  7.4 0.0 copy-start.5
  7.4 0.7 copy-done.5
  8.0 0.0 copy-start.6
  8.0 0.7 copy-done.6
  8.7 0.0 copy-start.7
  8.7 0.7 copy-done.7
  9.4 0.0 copy-start.8
  9.4 0.7 copy-done.8
  10.1 0.0 copy-start.9
  10.1 0.7 copy-done.9
  10.7 64.7 %shard_map.140 = (bf16[4,8192]{1,0:T(4,128)(2,1)S(1)}, bf16[4,896]{1,0:T(4,128)(2,1)S(1)}) custom-call(s32[1,4]{1,0:T(1,128)S(1)} %copy-done.8, s32[1,4]{1,0:T(1,128)S(1)} %copy-done.9, s32[4,8]{1,0:T(4,128)S(1)} %copy-done.6, f32[4,8]{1,0:T(4,128)S(1)} %copy-done.7, bf16[4,16,512]{2,1,0:T(8,128)(2,1)S(1)} %copy-done.2, bf16[4,1024]{1,0:T(4,128)(2,1)S(1)} %copy-done.3, ...), custom_call_target="tpu_custom_call" | custom-call | tf_op jit(solution)/shard_map/pallas_call | solution.py:466
  75.4 0.6 copy.17
  76.0 0.6 copy.18
Async XLA Ops:
  1.9 2.0 %copy-start = (bf16[1,7168,256]{2,1,0:T(8,128)(2,1)S(1)}, bf16[1,7168,256]{2,1,0:T(8,128)(2,1)}, u32[]{:S(2)}) copy-start(bf16[1,7168,256]{2,1,0:T(8,128)(2,1)} %wg_hbm.1) | copy-start | bytes 11010052
  3.9 1.2 %copy-start.1 = (bf16[4,256,512]{2,1,0:T(8,128)(2,1)S(1)}, bf16[4,256,512]{2,1,0:T(8,128)(2,1)}, u32[]{:S(2)}) copy-start(bf16[4,256,512]{2,1,0:T(8,128)(2,1)} %lat_hbm.1) | copy-start | bytes 3145732
  5.1 0.8 %copy-start.2 = (bf16[4,16,512]{2,1,0:T(8,128)(2,1)S(1)}, bf16[4,16,512]{2,1,0:T(8,128)(2,1)}, u32[]{:S(2)}) copy-start(bf16[4,16,512]{2,1,0:T(8,128)(2,1)} %q_ref.1) | copy-start | bytes 196612
  6.0 0.7 copy-start.3
  6.7 0.7 copy-start.4
  7.4 0.7 copy-start.5
  8.0 0.7 copy-start.6
  8.7 0.7 copy-start.7
  9.4 0.7 copy-start.8
  10.1 0.7 copy-start.9

commit v3 on v2

--- a/solution.py
+++ b/solution.py
@@ -21,6 +21,8 @@
 POS = 256
 CAP = 3
 SLOTS = NX * NZ * CAP
+SENDS = 48
+RECVS = 57
 FEAT = D // NE
 FF = 256
 
@@ -57,22 +59,23 @@
 
 
 class Gather:
-    def __init__(self, buf, send, recv, x, z, e):
-        self.buf, self.send, self.recv = buf, send, recv
+    def __init__(self, buf, start, sems, x, z, e):
+        self.buf, self.start_copy, self.sems = buf, start, sems
         self.x, self.z, self.e = x, z, e
-        self.copies = {}
+        self.second = {}
 
     def put(self, origin, hop, sign, low):
         block = self.buf.at[lax.rem(self.z + 2 * NZ - sign * origin, NZ), pl.ds(low, 2)]
         peer = (self.x * NZ + lax.rem(self.z + 2 * NZ + sign * hop, NZ), self.e)
-        n = len(self.copies)
-        copy = remote(block, block, self.send.at[n], self.recv.at[n], peer)
-        copy.start()
-        self.copies[origin + hop, sign, low] = copy
-
-    def start(self):
+        if origin + hop == 2:
+            sem = self.sems[len(self.second)]
+            self.second[sign, low] = self.start_copy(block, block, sem, peer)
+        else:
+            self.start_copy(block, block, self.sems[4], peer)
+
+    def start(self, lows=(0, 2)):
         for hop in (2, 1):
-            for low in (0, 2):
+            for low in lows:
                 for sign in (1, -1):
                     self.put(0, hop, sign, low)
 
@@ -80,19 +83,17 @@
         for first in (True, False):
             for sign in (1, -1):
                 low = 0 if first == (sign == 1) else 2
-                self.copies[2, sign, low].wait_recv()
+                self.second[sign, low].wait_recv()
                 if first:
                     self.put(2, 2, sign, low)
                 self.put(2, 1, sign, low)
 
     def finish(self):
-        for (distance, sign, low), copy in self.copies.items():
-            if distance != 2:
-                copy.wait_recv()
-
-    def drain(self):
-        for copy in self.copies.values():
-            copy.wait_send()
+        arrived(self.sems[4], self.buf.at[pl.ds(0, 5)])
+
+
+def arrived(sem, blocks):
+    pltpu.make_async_copy(blocks, blocks, sem).wait()
 
 
 def three_parts(level, side):
@@ -122,19 +123,18 @@
 
 
 def layer_kernel(
-    owner_ref, length_ref, routes_ref, combine_ref,
-    q_ref, qr_ref, tok_ref, gain_ref, rope_ref,
+    owner_hbm, length_hbm, routes_hbm, combine_hbm,
+    q_hbm, qr_hbm, tok_hbm, gain_hbm, rope_hbm,
     lat_hbm, wg_hbm, wu_hbm, wd_hbm,
-    att_ref, moe_ref,
-    table, wg, wu, wd, lat, kcat, qz, xbuf, xsend, qall, xt, tall, xn, opart, osib, omine, oin,
-    ysib, ysr, yown, ysend, yrecv, tw, xrs, xrr, zs, zr, og, oxs, oxr, af,
+    att_hbm, moe_hbm,
+    att_ref, moe_ref, owner_ref, length_ref, routes_ref, combine_ref, qr_ref, tok_ref, gain_ref, rope_ref, ropef, table, wg, wu, wd, lat, kcat, qz, xbuf0, xbuf1, xbuf2, xbuf3, xsend, qall, xt, tall, xn, opart, osib, omine, oin,
+    ysib, ysr, yown, ysend, yrecv, tw, xrs, xrr, zs, zr, og, oxs, oxr,
     tokf, tokb, tk, gall, mzs, mzr, mxs, mxr, mrow, owz, owx, tbl, phi, plo,
-    w_sem, t_sem, mz_s, mz_r, oz_s, oz_r, kz_s, kz_r, mx_s, mx_r, wx_s, wx_r, kx_s, kx_r, g_s, g_r,
-    qz_s, qz_r, qx_s, qx_r, qy_s, qy_r, qk_s, qk_r, ty_s, ty_r, tk_s, tk_r,
-    os_s, os_r, o_s, o_r, yk_s, yk_r, yy_s, yy_r, xr_s, xr_r, zr_s, zr_r, og_s, og_r, ox_s, ox_r,
+    w_sem, s_sem, t_sem, out_sem, send_sems, recv_sems,
 ):
     c, e, x, z, y, k = coordinates()
     pending = []
+    xbuf = (xbuf0, xbuf1, xbuf2, xbuf3)
 
     def zp(d):
         return (x * NZ + lax.rem(z + d, NZ), e)
@@ -150,11 +150,24 @@
 
     sib = (c, y * 2 + 1 - k)
 
-    def start(src, dst, send_sem, recv_sem, peer):
-        copy = remote(src, dst, send_sem, recv_sem, peer)
+    def start(src, dst, recv_sem, peer):
+        n = len(pending)
+        if n >= SENDS:
+            pending[n - SENDS].wait_send()
+        copy = remote(src, dst, send_sems.at[n % SENDS], recv_sem, peer)
         copy.start()
         pending.append(copy)
         return copy
+
+    taken = [0]
+
+    def take(count):
+        taken[0] += count
+        return [recv_sems.at[taken[0] - count + n] for n in range(count)]
+
+    oz_r, mz_r, kz_r, wx_r, mx_r, kx_r, g_r, tk_r, ox_r, yy_r, xr_r, zr_r = take(12)
+    qx_r, qk_r, os_r, o_r, yk_r = (take(4) for _ in range(5))
+    ty_r, qy_r, gather_r, back_r = take(3), take(12), take(5), take(5)
 
     loads = [
         pltpu.make_async_copy(lat_hbm, lat, w_sem.at[0]),
@@ -162,12 +175,22 @@
         pltpu.make_async_copy(wu_hbm.at[0], wu, w_sem.at[2]),
         pltpu.make_async_copy(wd_hbm.at[0], wd, w_sem.at[3]),
     ]
+    blocks = (
+        (routes_hbm, routes_ref), (combine_hbm, combine_ref), (owner_hbm, owner_ref), (length_hbm, length_ref),
+        (qr_hbm, qr_ref), (q_hbm, qz.at[z, :, :, pl.ds(0, LAT)]), (tok_hbm, tok_ref), (gain_hbm, gain_ref),
+        (rope_hbm, rope_ref),
+    )
+    small = [pltpu.make_async_copy(src, dst, s_sem.at[n]) for n, (src, dst) in enumerate(blocks)]
+    for load in small:
+        load.start()
     loads[0].start()
     wait_for_all = greet(
         [zp(d) for d in range(1, NZ)] + [xp(d) for d in range(1, NX)] + [ep(d) for d in range(1, NE)]
     )
     for load in loads[1:]:
         load.start()
+    for load in small[:-1]:
+        load.wait()
 
     lane = iota((8, 128), 1)
     mine = jnp.zeros((8, 128), jnp.int32)
@@ -190,7 +213,6 @@
     tokf[12:16, 128:256] = jnp.zeros((4, 128), F32)
     tokb[...] = tokf[...].astype(BF)
     gall[e] = gain_ref[...]
-    qz[z, :, :, 0:LAT] = q_ref[...]
     turned = jnp.concatenate(
         [
             jnp.where(
@@ -207,16 +229,33 @@
 
     wait_for_all()
     around = (1, 7, 2, 6, 3, 5, 4)
-    oz = [start(owz.at[z], owz.at[z], oz_s.at[d - 1], oz_r.at[d - 1], zp(d)) for d in around]
-    mz = [
-        start(mzs.at[lax.rem(z + d, NZ)], mzr.at[z], mz_s.at[d - 1], mz_r.at[d - 1], zp(d)) for d in around
-    ]
-    kz = [start(tokb, tk.at[x, z], kz_s.at[d - 1], kz_r.at[d - 1], zp(d)) for d in around]
-    gather = Gather(qz, qz_s, qz_r, x, z, e)
+    for d in around:
+        start(owz.at[z], owz.at[z], oz_r, zp(d))
+    for d in around:
+        start(mzs.at[lax.rem(z + d, NZ)], mzr.at[z], mz_r, zp(d))
+    for d in around:
+        start(tokb, tk.at[x, z], kz_r, zp(d))
+    gather = Gather(qz, start, gather_r, x, z, e)
     gather.start()
-    gains = [start(gain_ref, gall.at[e], g_s.at[d - 1], g_r.at[d - 1], ep(d)) for d in range(1, NE)]
+    for d in range(1, NE):
+        start(gain_ref, gall.at[e], g_r, ep(d))
     mzr[z] = mzs[z]
     tk[x, z] = tokb[...]
+
+    small[-1].wait()
+    for t in range(POS // 2):
+        ropef[:, t, :] = rope_ref[:, t * 128:(t + 1) * 128].astype(F32)
+    position = iota((POS, POS // 2), 0)
+    pair = iota((POS, POS // 2), 1) * 2
+    even = (position == pair).astype(F32).astype(BF)
+    odd = (position == pair + 1).astype(F32).astype(BF)
+    low = iota((POS // 2, 128), 1) < ROPE
+    for j in range(REQ):
+        rows = ropef[j]
+        near = jnp.where(low, rows, 0.0).astype(BF)
+        far = jnp.where(low, pltpu.roll(rows, ROPE, 1), 0.0).astype(BF)
+        turned = jnp.dot(even, near, preferred_element_type=F32) + jnp.dot(odd, far, preferred_element_type=F32)
+        kcat[j, :, LAT:] = turned.astype(BF)
 
     loads[0].wait()
     for j in range(REQ):
@@ -226,22 +265,23 @@
             scale = scale.astype(F32)
             packed = (block / scale).astype(BF)
             kcat[j, :, b * BLK:(b + 1) * BLK] = (packed.astype(F32) * scale).astype(BF)
-        kcat[j, :, LAT:] = rope_ref[j]
-
-    for copy in oz + mz:
-        copy.wait_recv()
+
+    arrived(oz_r, owz.at[pl.ds(0, NZ - 1)])
+    arrived(mz_r, mzr.at[pl.ds(0, NZ - 1)])
     owx[x] = functools.reduce(jnp.add, [owz[d] for d in range(NZ)])
     mxs[...] = functools.reduce(jnp.add, [mzr[d] for d in range(NZ)])
     mxr[x] = mxs[...]
-    wx = [start(owx.at[x], owx.at[x], wx_s.at[d - 1], wx_r.at[d - 1], xp(d)) for d in range(1, NX)]
-    mx = [start(mxs, mxr.at[x], mx_s.at[d - 1], mx_r.at[d - 1], xp(d)) for d in range(1, NX)]
-    for copy in kz:
-        copy.wait_recv()
-    kx = [start(tk.at[x], tk.at[x], kx_s.at[d - 1], kx_r.at[d - 1], xp(d)) for d in range(1, NX)]
+    for d in range(1, NX):
+        start(owx.at[x], owx.at[x], wx_r, xp(d))
+    for d in range(1, NX):
+        start(mxs, mxr.at[x], mx_r, xp(d))
+    arrived(kz_r, tk.at[0, pl.ds(0, NZ - 1)])
+    for d in range(1, NX):
+        start(tk.at[x], tk.at[x], kx_r, xp(d))
     gather.forward()
 
-    for copy in wx + mx:
-        copy.wait_recv()
+    arrived(wx_r, owx.at[pl.ds(0, NX - 1)])
+    arrived(mx_r, mxr.at[pl.ds(0, NX - 1)])
     sub = iota((128, 128), 0)
     col = iota((128, 128), 1)
     owners = functools.reduce(jnp.add, [owx[d] for d in range(NX)])[0:1, :]
@@ -270,8 +310,7 @@
     widen = (token_of == iota((128, 512), 0)).astype(F32).astype(BF)
     placing = jnp.dot(placing.astype(BF), widen, preferred_element_type=F32)
     group = jnp.bitwise_and(jnp.right_shift(iota((SLOTS, 512), 1), 2), 3)
-    for copy in kx:
-        copy.wait_recv()
+    arrived(kx_r, tk.at[pl.ds(0, NX - 1)])
     states = tk[...].reshape(512, 256)
     for g in range(4):
         width = 256 if g < 3 else 128
@@ -280,46 +319,43 @@
             part, states[:, 0:width], preferred_element_type=F32
         ).astype(BF)
 
-    ty = [start(xt, tall.at[e], ty_s.at[d - 1], ty_r.at[d - 1], yp(d)) for d in range(1, NY)]
-    tc = [start(xt, tall.at[e], tk_s.at[0], tk_r.at[0], sib)]
+    ty = [start(xt, tall.at[e], ty_r[d - 1], yp(d)) for d in range(1, NY)]
+    start(xt, tall.at[e], tk_r, sib)
     tall[e] = xt[...]
 
     gather.finish()
     to_scalars.wait()
-    qx = []
-    for d in range(1, NX):
-        target = lax.rem(x + d, NX)
-        for j in range(REQ):
-            r = (target * NZ + z) * REQ + j
+    for j in range(REQ):
+        for d in range(1, NX):
+            r = (lax.rem(x + d, NX) * NZ + z) * REQ + j
             xsend[d - 1, j] = qz[bits(table[0, r], 0, NZ), bits(table[1, r], 0, REQ)]
-        qx.append(start(xsend.at[d - 1], xbuf.at[x], qx_s.at[d - 1], qx_r.at[d - 1], xp(d)))
-    for j in range(REQ):
+            start(xsend.at[d - 1, j], xbuf[j].at[x], qx_r[j], xp(d))
         r = c * REQ + j
-        xbuf[x, j] = qz[bits(table[0, r], 0, NZ), bits(table[1, r], 0, REQ)]
-
-    for copy in qx:
-        copy.wait_recv()
-    for j in range(REQ):
-        qall[j, e] = xbuf[bits(table[0, c * REQ + j], 3, NX), j]
-    own = qall.at[:, e]
-    qy = [start(own, own, qy_s.at[d - 1], qy_r.at[d - 1], yp(d)) for d in range(1, NY)]
-    qk = [start(own, own, qk_s.at[0], qk_r.at[0], sib)]
+        xbuf[j][x] = qz[bits(table[0, r], 0, NZ), bits(table[1, r], 0, REQ)]
+
+    qy = []
+    for j in range(REQ):
+        arrived(qx_r[j], xbuf[j].at[pl.ds(0, NX - 1)])
+        qall[j, e] = xbuf[j][bits(table[0, c * REQ + j], 3, NX)]
+        block = qall.at[j, e]
+        for d in range(1, NY):
+            qy.append(start(block, block, qy_r[j * 3 + d - 1], yp(d)))
+        start(block, block, qk_r[j], sib)
     for d in range(1, NY):
         ty[d - 1].wait_recv()
         other = lax.rem(y + NY - d, NY) * 2 + k
-        tc.append(start(tall.at[other], tall.at[other], tk_s.at[d], tk_r.at[d], sib))
-    for d in range(1, NY):
-        qy[d - 1].wait_recv()
-        other = lax.rem(y + NY - d, NY) * 2 + k
-        block = qall.at[:, other]
-        qk.append(start(block, block, qk_s.at[d], qk_r.at[d], sib))
-    for copy in qk:
-        copy.wait_recv()
+        start(tall.at[other], tall.at[other], tk_r, sib)
+    for j in range(REQ):
+        for d in range(1, NY):
+            qy[j * 3 + d - 1].wait_recv()
+            block = qall.at[j, lax.rem(y + NY - d, NY) * 2 + k]
+            start(block, block, qk_r[j], sib)
 
     lanes = iota((1, POS), 1) + e * POS
     side = iota((HD * NE, QW - LAT), 1)
     oc = []
     for j in range(REQ):
+        arrived(qk_r[j], qall.at[j, pl.ds(0, NY)])
         scores = lax.dot_general(
             qall[j].reshape(NE * HD, QW), kcat[j], (((1,), (1,)), ((), ())), preferred_element_type=F32
         )
@@ -334,10 +370,10 @@
         for core in range(2):
             opart[core, j, :, :, :LAT] = out[:, core]
             opart[core, j, :, :, LAT:] = tail[:, core]
-        oc.append(start(opart.at[1 - k, j], osib.at[j], os_s.at[j], os_r.at[j], sib))
-
-    for copy in tc + gains:
-        copy.wait_recv()
+        oc.append(start(opart.at[1 - k, j], osib.at[j], os_r[j], sib))
+
+    arrived(tk_r, tall.at[pl.ds(0, NY)])
+    arrived(g_r, gall.at[pl.ds(0, NE - 1)])
     squares = jnp.zeros((SLOTS, 1), F32)
     for g in range(NE):
         rows = tall[g].astype(F32)
@@ -354,10 +390,8 @@
         values, level = merge([opart[k, j].reshape(NY * HD, QW), osib[j].reshape(NY * HD, QW)])
         omine[:, j, :, :LAT] = values.astype(BF).reshape(NY, HD, LAT)
         omine[:, j, :, LAT:] = three_parts(level, side).reshape(NY, HD, QW - LAT)
-    oy = [
-        start(omine.at[lax.rem(y + d, NY)], oin.at[d - 1], o_s.at[d - 1], o_r.at[d - 1], yp(d))
-        for d in range(1, NY)
-    ]
+        for d in range(1, NY):
+            start(omine.at[lax.rem(y + d, NY), j], oin.at[d - 1, j], o_r[j], yp(d))
 
     for load in loads[1:]:
         load.wait()
@@ -375,28 +409,26 @@
     yk = []
     for d in range(NY):
         ysib[d] = project(lax.rem(y + d + 1, NY) * 2 + 1 - k).astype(BF)
-        yk.append(start(ysib.at[d], ysr.at[d], yk_s.at[d], yk_r.at[d], sib))
-    yy = []
+        yk.append(start(ysib.at[d], ysr.at[d], yk_r[d], sib))
     for d in range(NY):
         yown[d] = project(lax.rem(y + d + 1, NY) * 2 + k)
     for d in range(NY - 1):
         yk[d].wait_recv()
         ysend[d] = (yown[d] + ysr[d].astype(F32)).astype(BF)
-        yy.append(start(ysend.at[d], yrecv.at[d], yy_s.at[d], yy_r.at[d], yp(d + 1)))
-
-    for copy in oy:
-        copy.wait_recv()
-    for j in range(REQ):
+        start(ysend.at[d], yrecv.at[d], yy_r, yp(d + 1))
+
+    back = Gather(og, start, back_r, x, z, e)
+    for j in range(REQ):
+        arrived(o_r[j], oin.at[:, j])
         values, level = merge([omine[y, j]] + [oin[d, j] for d in range(NY - 1)])
         og[z, j] = values.astype(BF)
-    back = Gather(og, og_s, og_r, x, z, e)
-    back.start()
+        if j % 2 == 1:
+            back.start((j - 1,))
 
     yk[NY - 1].wait_recv()
     summed = yown[NY - 1] + ysr[NY - 1].astype(F32)
     back.forward()
-    for copy in yy:
-        copy.wait_recv()
+    arrived(yy_r, yrecv)
     for d in range(NY - 1):
         summed = summed + yrecv[d].astype(F32)
     rounded = summed.astype(BF)
@@ -404,12 +436,10 @@
     both = lax.dot_general(phi[...], rounded, first_rows, preferred_element_type=F32)
     both = both + lax.dot_general(plo[...], rounded, first_rows, preferred_element_type=F32)
     tw[...] = both.reshape(NX, 32, FEAT)
-    xr = []
     for d in range(1, NX):
         xrs[d - 1] = tw[lax.rem(x + d, NX)].astype(BF)
-        xr.append(start(xrs.at[d - 1], xrr.at[d - 1], xr_s.at[d - 1], xr_r.at[d - 1], xp(d)))
-    for copy in xr:
-        copy.wait_recv()
+        start(xrs.at[d - 1], xrr.at[d - 1], xr_r, xp(d))
+    arrived(xr_r, xrr)
     own = tw[x]
     for d in range(NX - 1):
         own = own + xrr[d].astype(F32)
@@ -417,66 +447,65 @@
         zs[t, 0:4, 0:512] = own[4 * t:4 * t + 4, 0:512]
         zs[t, 4:8, 0:384] = own[4 * t:4 * t + 4, 512:896]
         zs[t, 4:8, 384:512] = jnp.zeros((4, 128), F32)
-    zc = [
-        start(zs.at[lax.rem(z + d, NZ)], zr.at[d - 1], zr_s.at[d - 1], zr_r.at[d - 1], zp(d)) for d in around
-    ]
+    for d in around:
+        start(zs.at[lax.rem(z + d, NZ)], zr.at[d - 1], zr_r, zp(d))
 
     back.finish()
-    ox = []
     for d in range(1, NX):
         target = lax.rem(x + d, NX)
         for j in range(REQ):
             r = table[2, (target * NZ + z) * REQ + j]
             oxs[d - 1, j] = og[bits(r, 2, NZ), bits(r, 0, REQ)]
-        ox.append(start(oxs.at[d - 1], oxr.at[x], ox_s.at[d - 1], ox_r.at[d - 1], xp(d)))
+        start(oxs.at[d - 1], oxr.at[x], ox_r, xp(d))
     for j in range(REQ):
         r = table[2, c * REQ + j]
         oxr[x, j] = og[bits(r, 2, NZ), bits(r, 0, REQ)]
 
-    for copy in zc:
-        copy.wait_recv()
+    arrived(zr_r, zr)
     final = zs[z]
     for d in range(NZ - 1):
         final = final + zr[d]
-    moe_ref[:, 0:512] = final[0:4, :].astype(BF)
-    moe_ref[:, 512:896] = final[4:8, 0:384].astype(BF)
-
-    for copy in ox:
-        copy.wait_recv()
+    moe_ref[:, 0:512] = final[0:4, :]
+    moe_ref[:, 512:896] = final[4:8, 0:384]
+    moe_out = pltpu.make_async_copy(moe_ref, moe_hbm, out_sem.at[0])
+    moe_out.start()
+    att_out = pltpu.make_async_copy(att_ref, att_hbm, out_sem.at[1])
+
+    arrived(ox_r, oxr.at[pl.ds(0, NX - 1)])
     for j in range(REQ):
         values = oxr[bits(table[2, c * REQ + j], 5, NX), j].astype(F32)
         for h in range(HD):
-            af[j:j + 1, h * LAT:(h + 1) * LAT] = values[h:h + 1, :]
-    att_ref[...] = af[...].astype(BF)
-    for copy in pending:
+            att_ref[j:j + 1, h * LAT:(h + 1) * LAT] = values[h:h + 1, :]
+    att_out.start()
+    for copy in pending[-SENDS:]:
         copy.wait_send()
-    gather.drain()
-    back.drain()
+    moe_out.wait()
+    att_out.wait()
 
 
 def layer(owner, lengths, routes, combine, q, qr, tok, gain, rope, lat, wg, wu, wd):
-    vmem = pl.BlockSpec(memory_space=pltpu.VMEM)
-    smem = pl.BlockSpec(memory_space=pltpu.SMEM)
-    hbm = pl.BlockSpec(memory_space=pl.ANY)
+    hbm = pl.BlockSpec(memory_space=pltpu.HBM)
     dma = pltpu.SemaphoreType.DMA
     V = pltpu.VMEM
-    pairs = []
-    for count in (7, 7, 7, 3, 3, 3, 7, 14, 3, 3, 4, 3, 4, 4, 3, 4, 3, 3, 7, 14, 3):
-        pairs += [dma((count,)), dma((count,))]
     return pl.pallas_call(
         layer_kernel,
         out_shape=(
-            jax.ShapeDtypeStruct((REQ, HD * LAT), BF),
-            jax.ShapeDtypeStruct((REQ, FEAT), BF),
+            jax.ShapeDtypeStruct((REQ, HD * LAT), F32),
+            jax.ShapeDtypeStruct((REQ, FEAT), F32),
         ),
-        in_specs=[smem] * 4 + [vmem] * 5 + [hbm] * 4,
-        out_specs=(vmem, vmem),
+        in_specs=[hbm] * 13,
+        out_specs=(hbm, hbm),
         scratch_shapes=[
+            V((REQ, HD * LAT), F32), V((REQ, FEAT), F32),
+            pltpu.SMEM((1, REQ), jnp.int32), pltpu.SMEM((1, REQ), jnp.int32),
+            pltpu.SMEM((REQ, 8), jnp.int32), pltpu.SMEM((REQ, 8), F32),
+            V((REQ, HD * ROPE), BF), V((REQ, FEAT), BF), V((7, 128), F32), V((REQ, POS * ROPE), BF), V((REQ, POS // 2, 128), F32),
             pltpu.SMEM((8, 128), jnp.int32),
             V((D, FF), BF), V((D, FF), BF), V((FF, D), BF),
             V((REQ, POS, LAT), BF), V((REQ, POS, QW), BF),
             V((NZ, REQ, HD, QW), BF),
-            V((NX, REQ, HD, QW), BF), V((NX - 1, REQ, HD, QW), BF),
+            V((NX, HD, QW), BF), V((NX, HD, QW), BF), V((NX, HD, QW), BF), V((NX, HD, QW), BF),
+            V((NX - 1, REQ, HD, QW), BF),
             V((REQ, NE, HD, QW), BF),
             V((SLOTS, FEAT), BF), V((NE, SLOTS, FEAT), BF), V((NE, SLOTS, FEAT), BF),
             V((2, REQ, NY, HD, QW), BF), V((REQ, NY, HD, QW), BF),
@@ -488,17 +517,16 @@
             V((NZ, 8, 512), F32), V((NZ - 1, 8, 512), F32),
             V((NZ, REQ, HD, LAT), BF),
             V((NX - 1, REQ, HD, LAT), BF), V((NX, REQ, HD, LAT), BF),
-            V((REQ, HD * LAT), F32),
             V((16, 256), F32), V((16, 256), BF), V((NX, NZ, 16, 256), BF),
             V((NE, 7, 128), F32),
             V((NZ, 8, 128), F32), V((NZ, 8, 128), F32),
             V((8, 128), F32), V((NX, 8, 128), F32), V((8, 128), F32),
             V((NZ, 8, 128), jnp.int32), V((NX, 8, 128), jnp.int32), V((8, 128), jnp.int32),
             V((SLOTS, 128), BF), V((SLOTS, 128), BF),
-            dma((4,)), dma((1,)),
-        ] + pairs,
+            dma((4,)), dma((9,)), dma((1,)), dma((2,)), dma((SENDS,)), dma((RECVS,)),
+        ],
         compiler_params=pltpu.CompilerParams(
-            collective_id=0, has_side_effects=True, vmem_limit_bytes=48 * 1024 * 1024
+            collective_id=0, has_side_effects=True, vmem_limit_bytes=64 * 1024 * 1024
         ),
     )(owner, lengths, routes, combine, q, qr, tok, gain, rope, lat, wg, wu, wd)
 
@@ -518,11 +546,11 @@
     up_weight,
     down_weight,
 ):
-    rope = jnp.pad(latent_rope.reshape(REQ, POS, ROPE), ((0, 0), (0, 0), (0, QW - LAT - ROPE)))
-    return layer(
+    attended, summed = layer(
         owner, lengths, routes, combine, query_plane, query_rope, decode_hidden,
-        norm_gain.reshape(7, 128), rope, latent_plane, gate_weight, up_weight, down_weight,
+        norm_gain.reshape(7, 128), latent_rope, latent_plane, gate_weight, up_weight, down_weight,
     )
+    return attended.astype(BF), summed.astype(BF)
 
 
 def solution(mesh):

time: 77 us -> 65.4 us (0.85)
  local copies, waits for them, and re-layouts: 11.3 us -> 0 us
  Pallas kernels: 64.7 us -> 61 us
  other arithmetic: 0 us -> 2.87 us
    unnamed x22 -> x0, local copies, waits for them, and re-layouts: 10.1 us -> none
    pallas_call x1, Pallas kernels: 64.7 us -> 61 us  [layer(): pl.pallas_call(layer_kernel, out_shape=(jax.ShapeDtypeStruct((REQ, HD * L...]
    convert_element_type x0 -> x2, other arithmetic: none -> 2.87 us  [local(): return (attended.astype(BF), summed.astype(BF))]
    reshape x1 -> x0, local copies, waits for them, and re-layouts: 1.15 us -> none  [local(): latent_rope.reshape(REQ, POS, ROPE)]
where the time goes in v3:
time: 65.4 us; the launch traced here: 64.5 us
  Pallas kernels  61 us (93%)
  other arithmetic  2.87 us (4%)
    pallas_call x1, Pallas kernels, layer(): pl.pallas_call(layer_kernel, out_shape=(jax.ShapeDtypeStruct((REQ, HD * L...  61 us
    convert_element_type x2, other arithmetic, local(): return (attended.astype(BF), summed.astype(BF))  2.87 us

profile of v3, /device:TPU:1, one launch (start us, length us, event | category | flops | bytes accessed | tf_op | source)
XLA Modules:
  0.0 64.5 jit_solution(17882569341318005607)
XLA Ops:
  0.6 61.0 %shard_map.140 = (f32[4,8192]{1,0:T(4,128)}, f32[4,896]{1,0:T(4,128)}) custom-call(s32[1,4]{1,0:T(1,128)} %owner_hbm.1, s32[1,4]{1,0:T(1,128)} %length_hbm.1, s32[4,8]{1,0:T(4,128)} %routes_hbm.1, f32[4,8]{1,0:T(4,128)} %combine_hbm.1, bf16[4,16,512]{2,1,0:T(8,128)(2,1)} %q_hbm.1, bf16[4,1024]{1,0:T(4,128)(2,1)} %qr_hbm.1, bf16[4,896]{1,0:T(4,128)(2,1)} %tok_hbm.1, ...), custom_call_target="tpu_custom_call" | custom-call | tf_op jit(solution)/shard_map/pallas_call | solution.py:490
  61.6 1.6 %convert_element_type.6 = bf16[4,8192]{1,0:T(4,128)(2,1)} convert(f32[4,8192]{1,0:T(4,128)} %get-tuple-element.4) | non-fusion elementwise | flops 32768 | bytes 196608 | tf_op jit(solution)/shard_map/convert_element_type | solution.py:553
  63.2 1.3 %convert_element_type.7 = bf16[4,896]{1,0:T(4,128)(2,1)} convert(f32[4,896]{1,0:T(4,128)} %get-tuple-element.5) | non-fusion elementwise | flops 3584 | bytes 21504 | tf_op jit(solution)/shard_map/convert_element_type | solution.py:553

commit v4 on v3

--- a/solution.py
+++ b/solution.py
@@ -22,7 +22,8 @@
 CAP = 3
 SLOTS = NX * NZ * CAP
 SENDS = 48
-RECVS = 57
+RECVS = 69
+HALVES = ((0, 512), (512, 384))
 FEAT = D // NE
 FF = 256
 
@@ -127,7 +128,7 @@
     q_hbm, qr_hbm, tok_hbm, gain_hbm, rope_hbm,
     lat_hbm, wg_hbm, wu_hbm, wd_hbm,
     att_hbm, moe_hbm,
-    att_ref, moe_ref, owner_ref, length_ref, routes_ref, combine_ref, qr_ref, tok_ref, gain_ref, rope_ref, ropef, table, wg, wu, wd, lat, kcat, qz, xbuf0, xbuf1, xbuf2, xbuf3, xsend, qall, xt, tall, xn, opart, osib, omine, oin,
+    af, att_ref, moe_ref, owner_ref, length_ref, routes_ref, combine_ref, qr_ref, tok_ref, gain_ref, rope_ref, ropef, table, wg, wu, wd, lat, kcat, qz, xbuf0, xbuf1, xbuf2, xbuf3, xsend, qall, xt, tall, xn, opart, osib, omine, oin,
     ysib, ysr, yown, ysend, yrecv, tw, xrs, xrr, zs, zr, og, oxs, oxr,
     tokf, tokb, tk, gall, mzs, mzr, mxs, mxr, mrow, owz, owx, tbl, phi, plo,
     w_sem, s_sem, t_sem, out_sem, send_sems, recv_sems,
@@ -165,9 +166,10 @@
         taken[0] += count
         return [recv_sems.at[taken[0] - count + n] for n in range(count)]
 
-    oz_r, mz_r, kz_r, wx_r, mx_r, kx_r, g_r, tk_r, ox_r, yy_r, xr_r, zr_r = take(12)
+    oz_r, mz_r, kz_r, wx_r, mx_r, kx_r, g_r, tk_r, ox_r = take(9)
+    yy_r, xr_r, zr_r = take(2), take(2), take(2)
     qx_r, qk_r, os_r, o_r, yk_r = (take(4) for _ in range(5))
-    ty_r, qy_r, gather_r, back_r = take(3), take(12), take(5), take(5)
+    ty_r, qy_r, gather_r, back_r = take(12), take(12), take(5), take(5)
 
     loads = [
         pltpu.make_async_copy(lat_hbm, lat, w_sem.at[0]),
@@ -312,15 +314,18 @@
     group = jnp.bitwise_and(jnp.right_shift(iota((SLOTS, 512), 1), 2), 3)
     arrived(kx_r, tk.at[pl.ds(0, NX - 1)])
     states = tk[...].reshape(512, 256)
+    ty = []
     for g in range(4):
         width = 256 if g < 3 else 128
         part = jnp.where(group == g, placing, 0.0).astype(BF)
+        columns = pl.ds(g * 256, width)
         xt[:, g * 256:g * 256 + width] = jnp.dot(
             part, states[:, 0:width], preferred_element_type=F32
         ).astype(BF)
-
-    ty = [start(xt, tall.at[e], ty_r[d - 1], yp(d)) for d in range(1, NY)]
-    start(xt, tall.at[e], tk_r, sib)
+        for d in range(1, NY):
+            ty.append(start(xt.at[:, columns], tall.at[e, :, columns], ty_r[g * 3 + d - 1], yp(d)))
+        start(xt.at[:, columns], tall.at[e, :, columns], tk_r, sib)
+
     tall[e] = xt[...]
 
     gather.finish()
@@ -341,10 +346,12 @@
         for d in range(1, NY):
             qy.append(start(block, block, qy_r[j * 3 + d - 1], yp(d)))
         start(block, block, qk_r[j], sib)
-    for d in range(1, NY):
-        ty[d - 1].wait_recv()
-        other = lax.rem(y + NY - d, NY) * 2 + k
-        start(tall.at[other], tall.at[other], tk_r, sib)
+    for g in range(4):
+        for d in range(1, NY):
+            ty[g * 3 + d - 1].wait_recv()
+            other = lax.rem(y + NY - d, NY) * 2 + k
+            block = tall.at[other, :, pl.ds(g * 256, 256 if g < 3 else 128)]
+            start(block, block, tk_r, sib)
     for j in range(REQ):
         for d in range(1, NY):
             qy[j * 3 + d - 1].wait_recv()
@@ -415,7 +422,10 @@
     for d in range(NY - 1):
         yk[d].wait_recv()
         ysend[d] = (yown[d] + ysr[d].astype(F32)).astype(BF)
-        start(ysend.at[d], yrecv.at[d], yy_r, yp(d + 1))
+    for h, (low, width) in enumerate(HALVES):
+        for d in range(NY - 1):
+            columns = pl.ds(low, width)
+            start(ysend.at[d, :, columns], yrecv.at[d, :, columns], yy_r[h], yp(d + 1))
 
     back = Gather(og, start, back_r, x, z, e)
     for j in range(REQ):
@@ -426,29 +436,33 @@
             back.start((j - 1,))
 
     yk[NY - 1].wait_recv()
-    summed = yown[NY - 1] + ysr[NY - 1].astype(F32)
+    first_rows = (((0,), (0,)), ((), ()))
     back.forward()
-    arrived(yy_r, yrecv)
-    for d in range(NY - 1):
-        summed = summed + yrecv[d].astype(F32)
-    rounded = summed.astype(BF)
-    first_rows = (((0,), (0,)), ((), ()))
-    both = lax.dot_general(phi[...], rounded, first_rows, preferred_element_type=F32)
-    both = both + lax.dot_general(plo[...], rounded, first_rows, preferred_element_type=F32)
-    tw[...] = both.reshape(NX, 32, FEAT)
-    for d in range(1, NX):
-        xrs[d - 1] = tw[lax.rem(x + d, NX)].astype(BF)
-        start(xrs.at[d - 1], xrr.at[d - 1], xr_r, xp(d))
-    arrived(xr_r, xrr)
-    own = tw[x]
-    for d in range(NX - 1):
-        own = own + xrr[d].astype(F32)
-    for t in range(NZ):
-        zs[t, 0:4, 0:512] = own[4 * t:4 * t + 4, 0:512]
-        zs[t, 4:8, 0:384] = own[4 * t:4 * t + 4, 512:896]
-        zs[t, 4:8, 384:512] = jnp.zeros((4, 128), F32)
-    for d in around:
-        start(zs.at[lax.rem(z + d, NZ)], zr.at[d - 1], zr_r, zp(d))
+    for h, (low, width) in enumerate(HALVES):
+        columns = pl.ds(low, width)
+        arrived(yy_r[h], yrecv.at[:, :, columns])
+        summed = yown[NY - 1, :, low:low + width] + ysr[NY - 1, :, low:low + width].astype(F32)
+        for d in range(NY - 1):
+            summed = summed + yrecv[d, :, low:low + width].astype(F32)
+        rounded = summed.astype(BF)
+        both = lax.dot_general(phi[...], rounded, first_rows, preferred_element_type=F32)
+        both = both + lax.dot_general(plo[...], rounded, first_rows, preferred_element_type=F32)
+        tw[:, :, low:low + width] = both.reshape(NX, 32, width)
+        for d in range(1, NX):
+            xrs[d - 1, :, low:low + width] = tw[lax.rem(x + d, NX), :, low:low + width].astype(BF)
+            start(xrs.at[d - 1, :, columns], xrr.at[d - 1, :, columns], xr_r[h], xp(d))
+    for h, (low, width) in enumerate(HALVES):
+        arrived(xr_r[h], xrr.at[:, :, pl.ds(low, width)])
+        own = tw[x, :, low:low + width]
+        for d in range(NX - 1):
+            own = own + xrr[d, :, low:low + width].astype(F32)
+        for t in range(NZ):
+            zs[h, t, 0:4, :] = own[4 * t:4 * t + 4, 0:256]
+            zs[h, t, 4:8, 0:width - 256] = own[4 * t:4 * t + 4, 256:width]
+            if width < 512:
+                zs[h, t, 4:8, width - 256:256] = jnp.zeros((4, 512 - width), F32)
+        for d in around:
+            start(zs.at[h, lax.rem(z + d, NZ)], zr.at[h, d - 1], zr_r[h], zp(d))
 
     back.finish()
     for d in range(1, NX):
@@ -461,12 +475,13 @@
         r = table[2, c * REQ + j]
         oxr[x, j] = og[bits(r, 2, NZ), bits(r, 0, REQ)]
 
-    arrived(zr_r, zr)
-    final = zs[z]
-    for d in range(NZ - 1):
-        final = final + zr[d]
-    moe_ref[:, 0:512] = final[0:4, :]
-    moe_ref[:, 512:896] = final[4:8, 0:384]
+    for h, (low, width) in enumerate(HALVES):
+        arrived(zr_r[h], zr.at[h])
+        final = zs[h, z]
+        for d in range(NZ - 1):
+            final = final + zr[h, d]
+        moe_ref[:, low:low + 256] = final[0:4, :].astype(BF)
+        moe_ref[:, low + 256:low + width] = final[4:8, 0:width - 256].astype(BF)
     moe_out = pltpu.make_async_copy(moe_ref, moe_hbm, out_sem.at[0])
     moe_out.start()
     att_out = pltpu.make_async_copy(att_ref, att_hbm, out_sem.at[1])
@@ -475,7 +490,8 @@
     for j in range(REQ):
         values = oxr[bits(table[2, c * REQ + j], 5, NX), j].astype(F32)
         for h in range(HD):
-            att_ref[j:j + 1, h * LAT:(h + 1) * LAT] = values[h:h + 1, :]
+            af[j:j + 1, h * LAT:(h + 1) * LAT] = values[h:h + 1, :]
+    att_ref[...] = af[...].astype(BF)
     att_out.start()
     for copy in pending[-SENDS:]:
         copy.wait_send()
@@ -490,13 +506,13 @@
     return pl.pallas_call(
         layer_kernel,
         out_shape=(
-            jax.ShapeDtypeStruct((REQ, HD * LAT), F32),
-            jax.ShapeDtypeStruct((REQ, FEAT), F32),
+            jax.ShapeDtypeStruct((REQ, HD * LAT), BF),
+            jax.ShapeDtypeStruct((REQ, FEAT), BF),
         ),
         in_specs=[hbm] * 13,
         out_specs=(hbm, hbm),
         scratch_shapes=[
-            V((REQ, HD * LAT), F32), V((REQ, FEAT), F32),
+            V((REQ, HD * LAT), F32), V((REQ, HD * LAT), BF), V((REQ, FEAT), BF),
             pltpu.SMEM((1, REQ), jnp.int32), pltpu.SMEM((1, REQ), jnp.int32),
             pltpu.SMEM((REQ, 8), jnp.int32), pltpu.SMEM((REQ, 8), F32),
             V((REQ, HD * ROPE), BF), V((REQ, FEAT), BF), V((7, 128), F32), V((REQ, POS * ROPE), BF), V((REQ, POS // 2, 128), F32),
@@ -514,7 +530,7 @@
             V((NY - 1, SLOTS, FEAT), BF), V((NY - 1, SLOTS, FEAT), BF),
             V((NX, 32, FEAT), F32),
             V((NX - 1, 32, FEAT), BF), V((NX - 1, 32, FEAT), BF),
-            V((NZ, 8, 512), F32), V((NZ - 1, 8, 512), F32),
+            V((2, NZ, 8, 256), F32), V((2, NZ - 1, 8, 256), F32),
             V((NZ, REQ, HD, LAT), BF),
             V((NX - 1, REQ, HD, LAT), BF), V((NX, REQ, HD, LAT), BF),
             V((16, 256), F32), V((16, 256), BF), V((NX, NZ, 16, 256), BF),
@@ -529,6 +545,22 @@
             collective_id=0, has_side_effects=True, vmem_limit_bytes=64 * 1024 * 1024
         ),
     )(owner, lengths, routes, combine, q, qr, tok, gain, rope, lat, wg, wu, wd)
+
+
+def hand_on_kernel(a_ref, b_ref, c_ref, d_ref):
+    c_ref[...] = a_ref[...]
+    d_ref[...] = b_ref[...]
+
+
+def hand_on(a, b):
+    hbm = pl.BlockSpec(memory_space=pltpu.VMEM)
+    return pl.pallas_call(
+        hand_on_kernel,
+        out_shape=(jax.ShapeDtypeStruct(a.shape, a.dtype), jax.ShapeDtypeStruct(b.shape, b.dtype)),
+        in_specs=[hbm, hbm],
+        out_specs=(hbm, hbm),
+        compiler_params=pltpu.CompilerParams(vmem_limit_bytes=64 * 1024 * 1024),
+    )(a, b)
 
 
 def local(
@@ -550,7 +582,7 @@
         owner, lengths, routes, combine, query_plane, query_rope, decode_hidden,
         norm_gain.reshape(7, 128), latent_rope, latent_plane, gate_weight, up_weight, down_weight,
     )
-    return attended.astype(BF), summed.astype(BF)
+    return hand_on(attended, summed)
 
 
 def solution(mesh):

time: 65.4 us -> 62.4 us (0.954); the launches traced: 64.5 us -> 62.3 us
  other arithmetic: 2.87 us -> 0 us
    convert_element_type x2 -> x0, other arithmetic: 2.87 us -> none  [local(): return (attended.astype(BF), summed.astype(BF))]
    pallas_call x0 -> x1, Pallas kernels: none -> 1.48 us  [hand_on(): pl.pallas_call(hand_on_kernel, out_shape=(jax.ShapeDtypeStruct(a.shape, a...]
    pallas_call x1, Pallas kernels: 61 us -> 60.2 us  [layer(): pl.pallas_call(layer_kernel, out_shape=(jax.ShapeDtypeStruct((REQ, HD * L...]
where the time goes in v4:
time: 62.4 us; the launch traced here: 62.3 us
  Pallas kernels  61.6 us (99%)
  between operations  0.64 us (1%)
    pallas_call x1, Pallas kernels, layer(): pl.pallas_call(layer_kernel, out_shape=(jax.ShapeDtypeStruct((REQ, HD * L...  60.2 us
    pallas_call x1, Pallas kernels, hand_on(): pl.pallas_call(hand_on_kernel, out_shape=(jax.ShapeDtypeStruct(a.shape, a...  1.48 us

profile of v4, /device:TPU:1, one launch (start us, length us, event | category | flops | bytes accessed | tf_op | source)
XLA Modules:
  0.0 62.3 jit_solution(3864206038901079870)
XLA Ops:
  0.6 60.2 %shard_map.140 = (bf16[4,8192]{1,0:T(4,128)(2,1)}, bf16[4,896]{1,0:T(4,128)(2,1)}) custom-call(s32[1,4]{1,0:T(1,128)} %owner_hbm.1, s32[1,4]{1,0:T(1,128)} %length_hbm.1, s32[4,8]{1,0:T(4,128)} %routes_hbm.1, f32[4,8]{1,0:T(4,128)} %combine_hbm.1, bf16[4,16,512]{2,1,0:T(8,128)(2,1)} %q_hbm.1, bf16[4,1024]{1,0:T(4,128)(2,1)} %qr_hbm.1, ...), custom_call_target="tpu_custom_call" | custom-call | tf_op jit(solution)/shard_map/pallas_call | solution.py:506
  60.8 1.5 %shard_map.141 = (bf16[4,8192]{1,0:T(4,128)(2,1)}, bf16[4,896]{1,0:T(4,128)(2,1)}) custom-call(bf16[4,8192]{1,0:T(4,128)(2,1)} %get-tuple-element.4.a_ref, bf16[4,896]{1,0:T(4,128)(2,1)} %get-tuple-element.5.b_ref), custom_call_target="tpu_custom_call" | custom-call | tf_op jit(solution)/shard_map/pallas_call | solution.py:557

commit v5 on v4

--- a/solution.py
+++ b/solution.py
@@ -22,7 +22,7 @@
 CAP = 3
 SLOTS = NX * NZ * CAP
 SENDS = 48
-RECVS = 69
+RECVS = 72
 HALVES = ((0, 512), (512, 384))
 FEAT = D // NE
 FF = 256
@@ -129,12 +129,13 @@
     lat_hbm, wg_hbm, wu_hbm, wd_hbm,
     att_hbm, moe_hbm,
     af, att_ref, moe_ref, owner_ref, length_ref, routes_ref, combine_ref, qr_ref, tok_ref, gain_ref, rope_ref, ropef, table, wg, wu, wd, lat, kcat, qz, xbuf0, xbuf1, xbuf2, xbuf3, xsend, qall, xt, tall, xn, opart, osib, omine, oin,
-    ysib, ysr, yown, ysend, yrecv, tw, xrs, xrr, zs, zr, og, oxs, oxr,
+    ysib, ysr, yown, ysend, yrecv, tw, xrs, xrr, zs, zr, og, oxs, oxr0, oxr1, oxr2, oxr3,
     tokf, tokb, tk, gall, mzs, mzr, mxs, mxr, mrow, owz, owx, tbl, phi, plo,
     w_sem, s_sem, t_sem, out_sem, send_sems, recv_sems,
 ):
     c, e, x, z, y, k = coordinates()
     pending = []
+    oxr = (oxr0, oxr1, oxr2, oxr3)
     xbuf = (xbuf0, xbuf1, xbuf2, xbuf3)
 
     def zp(d):
@@ -166,9 +167,9 @@
         taken[0] += count
         return [recv_sems.at[taken[0] - count + n] for n in range(count)]
 
-    oz_r, mz_r, kz_r, wx_r, mx_r, kx_r, g_r, tk_r, ox_r = take(9)
+    oz_r, mz_r, kz_r, wx_r, mx_r, kx_r, g_r, tk_r = take(8)
     yy_r, xr_r, zr_r = take(2), take(2), take(2)
-    qx_r, qk_r, os_r, o_r, yk_r = (take(4) for _ in range(5))
+    qx_r, qk_r, os_r, o_r, yk_r, ox_r = (take(4) for _ in range(6))
     ty_r, qy_r, gather_r, back_r = take(12), take(12), take(5), take(5)
 
     loads = [
@@ -194,20 +195,20 @@
     for load in small[:-1]:
         load.wait()
 
-    lane = iota((8, 128), 1)
-    mine = jnp.zeros((8, 128), jnp.int32)
+    lane = iota((1, 128), 1)
+    mine = jnp.zeros((1, 128), jnp.int32)
     for j in range(REQ):
         mine = jnp.where(lane == c * REQ + j, owner_ref[0, j], mine)
     owz[z] = mine
-    row = iota((64, 128), 0)
-    expert = jnp.bitwise_and(row, 7) * NZ + jnp.right_shift(row, 3)
-    wide = iota((64, 128), 1)
-    weights = jnp.zeros((64, 128), F32)
+    row = iota((32, 128), 0)
+    expert = jnp.bitwise_and(row, 3) * NZ + jnp.right_shift(row, 2)
+    wide = iota((32, 128), 1)
+    weights = jnp.zeros((32, 128), F32)
     for j in range(REQ):
         for n in range(8):
             hit = (expert == routes_ref[j, n]) & (wide == c * REQ + j)
             weights = jnp.where(hit, combine_ref[j, n], weights)
-    mzs[...] = weights.reshape(8, 8, 128)
+    mzs[...] = weights.reshape(NZ, NX, 128)
     state = tok_ref[...].astype(F32)
     for g in range(4):
         width = 256 if g < 3 else 128
@@ -286,7 +287,7 @@
     arrived(mx_r, mxr.at[pl.ds(0, NX - 1)])
     sub = iota((128, 128), 0)
     col = iota((128, 128), 1)
-    owners = functools.reduce(jnp.add, [owx[d] for d in range(NX)])[0:1, :]
+    owners = functools.reduce(jnp.add, [owx[d] for d in range(NX)])
     across = jnp.broadcast_to(owners, (128, 128))
     rank = jnp.sum(jnp.where((across.T == across) & (sub < col), 1, 0), axis=0, keepdims=True)
     place = jnp.broadcast_to(owners * REQ + rank, (128, 128)).T
@@ -465,15 +466,13 @@
             start(zs.at[h, lax.rem(z + d, NZ)], zr.at[h, d - 1], zr_r[h], zp(d))
 
     back.finish()
-    for d in range(1, NX):
-        target = lax.rem(x + d, NX)
-        for j in range(REQ):
-            r = table[2, (target * NZ + z) * REQ + j]
+    for j in range(REQ):
+        for d in range(1, NX):
+            r = table[2, (lax.rem(x + d, NX) * NZ + z) * REQ + j]
             oxs[d - 1, j] = og[bits(r, 2, NZ), bits(r, 0, REQ)]
-        start(oxs.at[d - 1], oxr.at[x], ox_r, xp(d))
-    for j in range(REQ):
+            start(oxs.at[d - 1, j], oxr[j].at[x], ox_r[j], xp(d))
         r = table[2, c * REQ + j]
-        oxr[x, j] = og[bits(r, 2, NZ), bits(r, 0, REQ)]
+        oxr[j][x] = og[bits(r, 2, NZ), bits(r, 0, REQ)]
 
     for h, (low, width) in enumerate(HALVES):
         arrived(zr_r[h], zr.at[h])
@@ -486,9 +485,9 @@
     moe_out.start()
     att_out = pltpu.make_async_copy(att_ref, att_hbm, out_sem.at[1])
 
-    arrived(ox_r, oxr.at[pl.ds(0, NX - 1)])
-    for j in range(REQ):
-        values = oxr[bits(table[2, c * REQ + j], 5, NX), j].astype(F32)
+    for j in range(REQ):
+        arrived(ox_r[j], oxr[j].at[pl.ds(0, NX - 1)])
+        values = oxr[j][bits(table[2, c * REQ + j], 5, NX)].astype(F32)
         for h in range(HD):
             af[j:j + 1, h * LAT:(h + 1) * LAT] = values[h:h + 1, :]
     att_ref[...] = af[...].astype(BF)
@@ -532,12 +531,12 @@
             V((NX - 1, 32, FEAT), BF), V((NX - 1, 32, FEAT), BF),
             V((2, NZ, 8, 256), F32), V((2, NZ - 1, 8, 256), F32),
             V((NZ, REQ, HD, LAT), BF),
-            V((NX - 1, REQ, HD, LAT), BF), V((NX, REQ, HD, LAT), BF),
+            V((NX - 1, REQ, HD, LAT), BF), V((NX, HD, LAT), BF), V((NX, HD, LAT), BF), V((NX, HD, LAT), BF), V((NX, HD, LAT), BF),
             V((16, 256), F32), V((16, 256), BF), V((NX, NZ, 16, 256), BF),
             V((NE, 7, 128), F32),
-            V((NZ, 8, 128), F32), V((NZ, 8, 128), F32),
-            V((8, 128), F32), V((NX, 8, 128), F32), V((8, 128), F32),
-            V((NZ, 8, 128), jnp.int32), V((NX, 8, 128), jnp.int32), V((8, 128), jnp.int32),
+            V((NZ, NX, 128), F32), V((NZ, NX, 128), F32),
+            V((NX, 128), F32), V((NX, NX, 128), F32), V((NX, 128), F32),
+            V((NZ, 1, 128), jnp.int32), V((NX, 1, 128), jnp.int32), V((8, 128), jnp.int32),
             V((SLOTS, 128), BF), V((SLOTS, 128), BF),
             dma((4,)), dma((9,)), dma((1,)), dma((2,)), dma((SENDS,)), dma((RECVS,)),
         ],

time: 62.4 us -> 61.5 us (0.986)
  Pallas kernels: 61.6 us -> 60.7 us
    pallas_call x1, Pallas kernels: 60.2 us -> 59.3 us  [layer(): pl.pallas_call(layer_kernel, out_shape=(jax.ShapeDtypeStruct((REQ, HD * L...]
where the time goes in v5:
time: 61.5 us; the launch traced here: 61.4 us
  Pallas kernels  60.7 us (99%)
  between operations  0.64 us (1%)
    pallas_call x1, Pallas kernels, layer(): pl.pallas_call(layer_kernel, out_shape=(jax.ShapeDtypeStruct((REQ, HD * L...  59.3 us
    pallas_call x1, Pallas kernels, hand_on(): pl.pallas_call(hand_on_kernel, out_shape=(jax.ShapeDtypeStruct(a.shape, a...  1.48 us

profile of v5, /device:TPU:1, one launch (start us, length us, event | category | flops | bytes accessed | tf_op | source)
XLA Modules:
  0.0 61.4 jit_solution(18403443462261388930)
XLA Ops:
  0.6 59.3 %shard_map.140 = (bf16[4,8192]{1,0:T(4,128)(2,1)}, bf16[4,896]{1,0:T(4,128)(2,1)}) custom-call(s32[1,4]{1,0:T(1,128)} %owner_hbm.1, s32[1,4]{1,0:T(1,128)} %length_hbm.1, s32[4,8]{1,0:T(4,128)} %routes_hbm.1, f32[4,8]{1,0:T(4,128)} %combine_hbm.1, bf16[4,16,512]{2,1,0:T(8,128)(2,1)} %q_hbm.1, bf16[4,1024]{1,0:T(4,128)(2,1)} %qr_hbm.1, ...), custom_call_target="tpu_custom_call" | custom-call | tf_op jit(solution)/shard_map/pallas_call | solution.py:505
  59.9 1.5 %shard_map.141 = (bf16[4,8192]{1,0:T(4,128)(2,1)}, bf16[4,896]{1,0:T(4,128)(2,1)}) custom-call(bf16[4,8192]{1,0:T(4,128)(2,1)} %get-tuple-element.4.a_ref, bf16[4,896]{1,0:T(4,128)(2,1)} %get-tuple-element.5.b_ref), custom_call_target="tpu_custom_call" | custom-call | tf_op jit(solution)/shard_map/pallas_call | solution.py:556
